TPU v7x, 512 devices: a whole 4x8x8 slice. The times are simulated.
512 devices in a mesh: sx: 16 (over z_lo, y), sy: 32 (over x, z_hi, core).
Axes of the slice: x: 4, y: 8, z: 8 (z_hi: 4, z_lo: 2; z = z_hi * 2 + z_lo), core: 2. Of those that a mesh axis runs over, the one named last changes fastest.
Arguments:
- forward_weights: float32 [4096, 8, 432], P(('sy', 'sx')), may hold values from -6 to 6
- adjoint_weights: float32 [32768, 432], P(('sx', 'sy')), may hold values from -6 to 6
- medium: float32 [4], replicated, may hold values from 0.2 to 0.6
Outputs:
- forward_out: float32 [32768, 432], P(('sx', 'sy'))
- adjoint_out: float32 [8, 4096, 432], P(None, ('sy', 'sx'))
All inputs are finite; a program needn't handle non-finite values.
Results may differ from a plain program's by a relative error of at most 0.0003.
Values sent between devices are 32-bit elements; how exact they have to be, the bound alone decides.
No kernel may reach another device: no remote copies, remote signals or barrier semaphores. Data moves between devices by JAX's collectives and lax.ppermute only.
A program may use at most 64 MiB of HBM per device.

v0:
```python
import math

import jax
import jax.numpy as jnp
import numpy as np
from jax import lax
from jax.sharding import Mesh
from jax.sharding import PartitionSpec as P

ORDER = 6
LEVELS = 4
Q = 216
SY = ("sy_0", "sy_1", "sy_2")
SY_SX = ("sy_0", "sy_1", "sy_2", "sx")
SX_SY = ("sx", "sy_0", "sy_1", "sy_2")


two_pi = 2.0 * math.pi
shrink = 1.0 / math.sqrt(8.0)
band = 8.0


def in_blocks(x, dim, size):
    dims = x.shape
    pieces = x.reshape(*dims[:dim], size, dims[dim] // size, *dims[dim + 1 :])
    return jnp.moveaxis(pieces, dim, 0)


def in_order(pieces, dim):
    pieces = jnp.moveaxis(pieces, 0, dim)
    dims = pieces.shape
    return pieces.reshape(*dims[:dim], dims[dim] * dims[dim + 1], *dims[dim + 2 :])


def exchange_in_order(pieces, axes, sequence):
    inside = pieces.shape[1:]
    result = pieces.reshape(*(lax.axis_size(a) for a in axes), *inside)
    for k in sequence:
        result = lax.all_to_all(result, axes[k], k, k, tiled=True)
    return result.reshape(-1, *inside)


def two_step_exchange(x, groups, sequence, split_dim, concat_dim):
    size = lax.axis_size(groups[0]) * lax.axis_size(groups[1])
    pieces = in_blocks(x, split_dim, size)
    return in_order(exchange_in_order(pieces, groups, sequence), concat_dim)


def cheb_points(order_count):
    return np.array(
        [
            (1.0 - math.cos((2 * node_index + 1) * math.pi / (2 * order_count))) / 2.0
            for node_index in range(order_count)
        ]
    )


def child_table(order_count):
    nodes_here = cheb_points(order_count)
    halves = []
    for offset_bit in range(2):
        matrix = np.zeros((order_count, order_count))
        for row_index in range(order_count):
            where_at = (nodes_here[row_index] + offset_bit) / 2.0
            for col_index in range(order_count):
                value_now = 1.0
                for other_index in range(order_count):
                    if other_index != col_index:
                        value_now *= (where_at - nodes_here[other_index]) / (
                            nodes_here[col_index] - nodes_here[other_index]
                        )
                matrix[row_index, col_index] = value_now
        halves.append(matrix)
    blocks_out = []
    for child_index in range(8):
        along_x = halves[child_index // 4]
        along_y = halves[child_index // 2 % 2]
        along_z = halves[child_index % 2]
        blocks_out.append(np.kron(np.kron(along_x, along_y), along_z))
    return jnp.asarray(np.stack(blocks_out), dtype=jnp.float32)


def box_digits(box_index, groups):
    coord_x = jnp.zeros_like(box_index)
    coord_y = jnp.zeros_like(box_index)
    coord_z = jnp.zeros_like(box_index)
    for group_now in range(groups):
        digit_now = box_index // 8 ** (groups - 1 - group_now) % 8
        coord_x = coord_x * 2 + digit_now // 4
        coord_y = coord_y * 2 + digit_now // 2 % 2
        coord_z = coord_z * 2 + digit_now % 2
    return jnp.stack([coord_x, coord_y, coord_z], axis=-1).astype(jnp.float32)


def box_centres(box_index, groups):
    return (box_digits(box_index, groups) + 0.5) / float(2**groups)


def box_points(box_index, groups):
    box_side = band / float(2**groups)
    nodes_here = jnp.asarray(cheb_points(ORDER), dtype=jnp.float32)
    grid_x = jnp.repeat(nodes_here, ORDER * ORDER)
    grid_y = jnp.tile(jnp.repeat(nodes_here, ORDER), ORDER)
    grid_z = jnp.tile(nodes_here, ORDER * ORDER)
    offsets = jnp.stack([grid_x, grid_y, grid_z], axis=-1)
    corner = box_digits(box_index, groups)
    return box_side * (corner[..., None, :] + offsets)


def phase_angle(centres, points, medium):
    along = jnp.sum(centres * points, axis=-1)
    radius = jnp.sqrt(jnp.sum(points * points, axis=-1))
    travel = medium[0] + jnp.sum(medium[1:] * centres, axis=-1)
    return two_pi * (along + travel * radius)


def complex_turn(real_part, imag_part, angle_now, sign_now):
    cosine = jnp.cos(angle_now)
    sine_part = sign_now * jnp.sin(angle_now)
    return (real_part * cosine - imag_part * sine_part, real_part * sine_part + imag_part * cosine)


def forward_level(weights, src_off, tgt_off, level_now, medium, interp):
    src_count, tgt_count = (weights.shape[0], weights.shape[1])
    shot_count, point_count = (weights.shape[3], weights.shape[4])
    parent_count = src_count // 8
    new_targets = tgt_off * 8 + jnp.arange(tgt_count * 8, dtype=jnp.int32)
    centres = box_centres(new_targets, level_now + 2).reshape(tgt_count, 8, 3)
    children = src_off + jnp.arange(src_count, dtype=jnp.int32)
    child_points = box_points(children, LEVELS - level_now).reshape(parent_count, 8, point_count, 3)
    parents = src_off // 8 + jnp.arange(parent_count, dtype=jnp.int32)
    parent_points = box_points(parents, LEVELS - level_now - 1)
    theta_in = phase_angle(
        centres[None, None, :, :, None, :], child_points[:, :, None, None, :, :], medium
    )
    theta_out = phase_angle(
        centres[None, :, :, None, :], parent_points[:, None, None, :, :], medium
    )
    shaped = weights.reshape(parent_count, 8, tgt_count, 1, 2, shot_count, point_count)
    turned = complex_turn(
        shaped[:, :, :, :, 0], shaped[:, :, :, :, 1], theta_in[:, :, :, :, None, :], 1.0
    )
    stacked = jnp.stack(turned, axis=4)
    mixed = jnp.einsum("pctkxhq,cqs->ptkxhs", stacked, interp, precision=lax.Precision.HIGHEST)
    result_re, result_im = complex_turn(
        mixed[:, :, :, 0], mixed[:, :, :, 1], theta_out[:, :, :, None, :], -1.0
    )
    output = shrink * jnp.stack([result_re, result_im], axis=3)
    return output.reshape(parent_count, tgt_count * 8, 2, shot_count, point_count)


def adjoint_level(values, tgt_off, src_off, level_now, medium, interp):
    tgt_count, src_count = (values.shape[0], values.shape[1])
    shot_count, point_count = (values.shape[3], values.shape[4])
    parent_count = tgt_count // 8
    targets = tgt_off + jnp.arange(tgt_count, dtype=jnp.int32)
    centres = box_centres(targets, level_now + 2).reshape(parent_count, 8, 3)
    sources = src_off + jnp.arange(src_count, dtype=jnp.int32)
    source_points = box_points(sources, LEVELS - level_now - 1)
    children = src_off * 8 + jnp.arange(src_count * 8, dtype=jnp.int32)
    child_points = box_points(children, LEVELS - level_now).reshape(src_count, 8, point_count, 3)
    theta_out = phase_angle(
        centres[:, :, None, None, :], source_points[None, None, :, :, :], medium
    )
    theta_in = phase_angle(
        centres[:, :, None, None, None, :], child_points[None, None, :, :, :, :], medium
    )
    shaped = values.reshape(parent_count, 8, src_count, 2, shot_count, point_count)
    turned = complex_turn(shaped[:, :, :, 0], shaped[:, :, :, 1], theta_out[:, :, :, None, :], 1.0)
    stacked = jnp.stack(turned, axis=3)
    spread = jnp.einsum("pkbxhs,cqs->pkbcxhq", stacked, interp, precision=lax.Precision.HIGHEST)
    back_re, back_im = complex_turn(
        spread[:, :, :, :, 0], spread[:, :, :, :, 1], theta_in[:, :, :, :, None, :], -1.0
    )
    output = shrink * jnp.stack([jnp.sum(back_re, axis=1), jnp.sum(back_im, axis=1)], axis=3)
    return output.reshape(parent_count, src_count * 8, 2, shot_count, point_count)


def flatten_pairs(array_now):
    return array_now.reshape(array_now.shape[0], array_now.shape[1], -1)


def unfold_pairs(array_now):
    return array_now.reshape(array_now.shape[0], array_now.shape[1], 2, -1, Q)


def forward_moved(state_in, moved_array, axis_index):
    array_now, src_off, tgt_off, level_now = state_in
    return (
        moved_array,
        src_off - axis_index * array_now.shape[0],
        tgt_off + axis_index * moved_array.shape[1],
        level_now,
    )


def adjoint_moved(state_in, moved_array, axis_index):
    array_now, tgt_off, src_off, level_now = state_in
    return (
        moved_array,
        tgt_off - axis_index * array_now.shape[0],
        src_off + axis_index * moved_array.shape[1],
        level_now,
    )


def forward_steps(state_in, operations, medium, interp, index_x):
    for operation in operations:
        array_now, src_off, tgt_off, level_now = state_in
        if operation == "level":
            state_in = (
                forward_level(array_now, src_off, tgt_off, level_now, medium, interp),
                src_off // 8,
                tgt_off * 8,
                level_now + 1,
            )
        else:
            moved_array = unfold_pairs(
                lax.all_to_all(
                    flatten_pairs(array_now), "sx", split_axis=1, concat_axis=0, tiled=True
                )
            )
            state_in = forward_moved(state_in, moved_array, index_x)
    return state_in


def adjoint_steps(state_in, operations, medium, interp, index_x):
    for operation in operations:
        array_now, tgt_off, src_off, level_now = state_in
        if operation == "level":
            state_in = (
                adjoint_level(array_now, tgt_off, src_off, level_now - 1, medium, interp),
                tgt_off // 8,
                src_off * 8,
                level_now - 1,
            )
        else:
            moved_array = unfold_pairs(
                lax.all_to_all(
                    flatten_pairs(array_now), "sx", split_axis=1, concat_axis=0, tiled=True
                )
            )
            state_in = adjoint_moved(state_in, moved_array, index_x)
    return state_in


def shards(forward_weights, adjoint_weights, medium):
    interp = child_table(ORDER)
    size_x = lax.axis_size("sx")
    size_y = lax.axis_size(SY)
    index_x = lax.axis_index("sx")
    index_y = lax.axis_index(SY)
    local_sources = forward_weights.shape[0]
    plan_ops = []
    remaining = [("sx", size_x), ("sy", size_y)]
    local_width = local_sources
    for level_now in range(LEVELS):
        while local_width < 8:
            axis_name, axis_size = remaining.pop(0)
            plan_ops.append(axis_name)
            local_width = local_width * axis_size
        plan_ops.append("level")
        local_width = local_width // 8
    cut_at = plan_ops.index("sy")
    early_ops = plan_ops[:cut_at]
    late_ops = plan_ops[cut_at + 1 :]
    forward_state = (
        unfold_pairs(forward_weights),
        (index_y * size_x + index_x) * local_sources,
        jnp.int32(0),
        0,
    )
    back_state = (
        unfold_pairs(adjoint_weights[:, None]),
        (index_x * size_y + index_y) * adjoint_weights.shape[0],
        jnp.int32(0),
        LEVELS,
    )
    forward_state = forward_steps(forward_state, early_ops, medium, interp, index_x)
    back_state = adjoint_steps(back_state, list(reversed(late_ops)), medium, interp, index_x)
    moved_forward, moved_back = (
        two_step_exchange(
            flatten_pairs(forward_state[0]), (("sy_0", "sy_1"), "sy_2"), (1, 0), 1, 0
        ),
        two_step_exchange(flatten_pairs(back_state[0]), (("sy_0", "sy_1"), "sy_2"), (1, 0), 1, 0),
    )
    forward_state = forward_moved(forward_state, unfold_pairs(moved_forward), index_y)
    back_state = adjoint_moved(back_state, unfold_pairs(moved_back), index_y)
    forward_state = forward_steps(forward_state, late_ops, medium, interp, index_x)
    back_state = adjoint_steps(back_state, list(reversed(early_ops)), medium, interp, index_x)
    forward_out = forward_state[0].reshape(forward_state[0].shape[1], -1)
    return (forward_out, flatten_pairs(back_state[0]))


def solution(mesh):
    split = Mesh(mesh.devices.reshape(mesh.shape["sx"], 4, 4, 2), ("sx", "sy_0", "sy_1", "sy_2"))
    return jax.shard_map(
        shards,
        mesh=split,
        in_specs=(P(SY_SX, None, None), P(SX_SY, None), P()),
        out_specs=(P(SX_SY, None), P(None, SY_SX, None)),
        check_vma=False,
    )
```

profile of v0, /device:TPU:2, one launch (start us, length us, event | category | flops | bytes accessed | tf_op | source)
XLA Modules:
  0.0 162.8 jit_solution(14685372909776085606)
XLA Ops:
  2.7 0.7 tile.98
  3.6 0.7 broadcast_in_dim.65
  4.6 0.7 broadcast_in_dim.64
  7.6 0.7 broadcast_multiply_fusion.1
  8.6 1.1 reshape_reshape_broadcast_in_dim.3
  10.9 0.7 multiply_reduce_fusion.8
  12.0 2.1 %convolution_bitcast_fusion.3 = f32[8,8,1,8,2,1,216]{6,1,4,0,3,5,2:T(8,128)S(1)} fusion(f32[8,216,216,1,1]{2,1,4,3,0:T(8,128)S(1)} %copy-done.1, f32[8,8,1,1,1,216]{5,1,3,0,4,2:T(8,128)S(1)} %get-tuple-element.31, f32[8,8,1,1,1,216]{5,1,3,0,4,2:T(8,128)S(1)} %get-tuple-element.30), kind=kOutput, calls=%fused_computation.11 | convolution fusion | flops 573336576 | bytes 2488320 | tf_op jit(solution)/shard_map/pkbxhs,cqs->pkbcxhq/dot_general | solution.py:171
  14.1 2.7 %subtract_reduce_fusion.3 = (f32[8,8,216]{2,0,1:T(8,128)S(1)}, f32[8,8,216]{2,0,1:T(8,128)S(1)}) fusion(f32[8,8,1,8,2,1,216]{6,1,4,0,3,5,2:T(8,128)S(1)} %convolution_bitcast_fusion.3, f32[8,8,8,216]{3,2,1,0:T(8,128)S(1)} %multiply_reduce_fusion.3, f32[8,216]{1,0:T(8,128)S(1)} %sqrt.137, f32[8,8]{1,0:T(8,128)S(1)} %broadcast_add_fusion.6), kind=kLoop, calls=%fused_computation.62 | loop fusion | flops 1299456 | bytes 1444864 | tf_op jit(solution)/shard_map/reduce_sum | solution.py:175
  18.2 2.1 %convolution_bitcast_fusion.2 = f32[1,8,8,8,2,1,216]{6,2,4,1,3,5,0:T(8,128)S(1)} fusion(f32[8,216,216,1,1]{2,1,4,3,0:T(8,128)S(1)} %copy-done.1, f32[1,8,8,1,1,216]{5,2,3,1,4,0:T(8,128)S(1)} %get-tuple-element.27, f32[1,8,8,1,1,216]{5,2,3,1,4,0:T(8,128)S(1)} %get-tuple-element.26), kind=kOutput, calls=%fused_computation.10 | convolution fusion | flops 573336576 | bytes 2488320 | tf_op jit(solution)/shard_map/pkbxhs,cqs->pkbcxhq/dot_general | solution.py:171
  20.3 2.5 %subtract_reduce_fusion.2 = (f32[8,8,216]{2,0,1:T(8,128)S(1)}, f32[8,8,216]{2,0,1:T(8,128)S(1)}) fusion(f32[1,8,8,8,2,1,216]{6,2,4,1,3,5,0:T(8,128)S(1)} %convolution_bitcast_fusion.2, f32[8,8,8,216]{3,2,1,0:T(8,128)S(1)} %multiply_reduce_fusion.2, f32[8,8,216]{2,0,1:T(8,128)S(1)} %copy.435, f32[8]{0:T(128)S(1)} %get-tuple-element.119), kind=kLoop, calls=%fused_computation.59 | loop fusion | flops 1299456 | bytes 1493024 | tf_op jit(solution)/shard_map/reduce_sum | solution.py:175
  23.2 3.8 %all_to_all.44 = f32[16,2,1,2,432]{4,3,0,2,1:T(2,128)S(1)} all-to-all(f32[16,2,1,2,432]{4,3,0,2,1:T(2,128)S(1)} %copy.439), channel_id=1, replica_groups=mesh['sx'=16,'sy_0'=4,'sy_1'=4,'sy_2'=2] {'sy_2'}, dimensions={1} | all-to-all | bytes 221184 | tf_op jit(solution)/shard_map/all_to_all | solution.py:39
  27.1 0.7 copy.440
  27.7 13.3 %all-to-all-start.4 = ((f32[16,2,1,2,432]{4,3,1,2,0:T(2,128)}), f32[16,2,1,2,432]{4,3,1,2,0:T(2,128)S(1)}, u32[]{:S(2)}, u32[]{:S(2)}) async-start(f32[16,2,1,2,432]{4,3,1,2,0:T(2,128)} %copy.440), calls=%async_computation.4 | async-start | bytes 262144 | tf_op jit(solution)/shard_map/all_to_all | solution.py:39
  49.4 0.7 copy.446
  50.4 0.7 multiply_reduce_fusion.23
  51.4 0.7 broadcast_add_fusion
  52.6 0.7 multiply_reduce_fusion.15
  54.5 0.7 multiply_reduce_fusion.24
  61.0 0.7 multiply_reduce_fusion.13
  61.9 2.0 %multiply_subtract_fusion.3 = (f32[1,8,8,8,1,1,216]{6,3,1,4,2,5,0:T(8,128)S(1)}, f32[1,8,8,8,1,1,216]{6,3,1,4,2,5,0:T(8,128)S(1)}) fusion(f32[8,8,8,216]{3,2,1,0:T(8,128)S(1)} %multiply_reduce_fusion.7, f32[8,8,216]{2,0,1:T(8,128)S(1)} %get-tuple-element.111, f32[8,216]{1,0:T(8,128)S(1)} %sqrt.128, f32[8,8]{1,0:T(8,128)S(1)} %broadcast_add_fusion.11, ...), kind=kLoop, calls=%fused_computation.71 | loop fusion | flops 995328 | bytes 1444864 | tf_op jit(solution)/shard_map/sub | solution.py:120
  64.0 1.4 convolution_bitcast_fusion.7
  65.8 1.0 mul.4774
  68.3 1.0 multiply_reduce_fusion.6
  69.3 0.7 multiply_reduce_fusion.16
  72.0 1.5 sqrt.132
  73.5 0.8 fusion.267
  74.8 0.7 sqrt.133
  75.6 1.3 sqrt.134
  76.9 0.8 fusion.69
  78.3 0.8 fusion.72
  81.3 0.7 multiply_reduce_fusion.9
  82.0 1.0 multiply_reduce_fusion.1
  83.1 0.8 fusion.270
  84.3 8.2 %all-to-all-start = ((f32[1,64,432]{2,0,1:T(1,128)}), f32[1,64,432]{2,0,1:T(1,128)}, u32[]{:S(2)}, u32[]{:S(2)}) async-start(f32[1,64,432]{2,0,1:T(1,128)} %mul.4774), calls=%async_computation | async-start | bytes 262144 | tf_op jit(solution)/shard_map/all_to_all | solution.py:219
  92.5 0.9 reshape_reshape_reshape_reshape.7
  93.4 1.7 %fusion.428 = (f32[4,8,2,1,1,216]{5,3,2,1,0,4:T(1,128)}, f32[4,8,2,1,1,216]{5,3,2,1,0,4:T(1,128)}) fusion(f32[4,8,2,2,1,216]{5,3,2,1,0,4:T(2,128)} %reshape_reshape_reshape_reshape.7), kind=kLoop, calls=%fused_computation.1350 | loop fusion | bytes 221184 | tf_op jit(solution)/shard_map/slice | solution.py:169
  95.1 6.0 %all-to-all-done = f32[1,64,432]{2,0,1:T(1,128)} async-done(((f32[1,64,432]{2,0,1:T(1,128)}), f32[1,64,432]{2,0,1:T(1,128)}, u32[]{:S(2)}, u32[]{:S(2)}) %all-to-all-start) | async-done | bytes 110624 | tf_op jit(solution)/shard_map/all_to_all | solution.py:219
  101.1 1.9 %reduce.52 = f32[64,432]{1,0:T(8,128)} reduce(f32[1,64,432]{2,0,1:T(1,128)} %all-to-all-done, f32[]{:T(128)} %constant.2451), dimensions={0}, to_apply=%all_to_all.30.reduce_sub_computation | reduce | bytes 221188 | tf_op jit(solution)/shard_map/all_to_all | solution.py:219
  103.0 1.1 reshape_reshape.7
  104.2 3.7 %multiply_subtract_fusion.2 = (f32[2,8,4,8,1,1,216]{6,3,1,4,2,0,5:T(8,128)S(1)}, f32[2,8,4,8,1,1,216]{6,3,1,4,2,0,5:T(8,128)S(1)}) fusion(f32[2,8,4,8,216]{4,3,2,1,0:T(8,128)} %multiply_reduce_fusion.6, f32[2,8,4,216]{3,1,2,0:T(8,128)S(1)} %bitcast.578, f32[2,8,216]{2,1,0:T(8,128)} %sqrt.130, f32[4,8]{1,0:T(4,128)} %broadcast_add_fusion.15, ...), kind=kLoop, calls=%fused_computation.69 | loop fusion | flops 995328 | bytes 1451648 | tf_op jit(solution)/shard_map/sub | solution.py:120
  108.0 1.4 convolution_bitcast_fusion.6
  109.9 0.8 mul.4489
  110.7 1.0 reshape.11716
  111.8 3.8 %all_to_all.45 = f32[16,2,2,1,432]{4,2,0,3,1:T(2,128)S(1)} all-to-all(f32[16,2,2,1,432]{4,2,0,3,1:T(2,128)S(1)} %copy.404), channel_id=1, replica_groups=mesh['sx'=16,'sy_0'=4,'sy_1'=4,'sy_2'=2] {'sy_2'}, dimensions={1} | all-to-all | bytes 221184 | tf_op jit(solution)/shard_map/all_to_all | solution.py:39
  115.6 0.7 copy.405
  116.3 9.8 %all-to-all-start.2 = ((f32[16,2,2,1,432]{4,2,1,3,0:T(2,128)}), f32[16,2,2,1,432]{4,2,1,3,0:T(2,128)S(1)}, u32[]{:S(2)}, u32[]{:S(2)}) async-start(f32[16,2,2,1,432]{4,2,1,3,0:T(2,128)} %copy.405), calls=%async_computation.2 | async-start | bytes 262144 | tf_op jit(solution)/shard_map/all_to_all | solution.py:39
  126.1 1.3 multiply_subtract_fusion.5
  127.4 3.5 %convolution_bitcast_fusion.1 = f32[4,8,2,8,2,1,216]{6,1,4,2,0,3,5:T(8,128)S(1)} fusion(f32[8,216,216,1,1,1]{2,1,5,4,3,0:T(8,128)} %constant.2449, f32[4,8,2,1,1,216]{5,1,3,2,0,4:T(8,128)S(1)} %get-tuple-element.37, f32[4,8,2,1,1,216]{5,1,3,2,0,4:T(8,128)S(1)} %get-tuple-element.36), kind=kOutput, calls=%fused_computation.9 | convolution fusion | flops 573336576 | bytes 2488320 | tf_op jit(solution)/shard_map/pkbxhs,cqs->pkbcxhq/dot_general | solution.py:171
  131.0 2.8 %subtract_reduce_fusion.1 = (f32[4,2,8,216]{3,1,0,2:T(2,128)S(1)}, f32[4,2,8,216]{3,1,0,2:T(2,128)S(1)}) fusion(f32[4,8,2,8,2,1,216]{6,1,4,2,0,3,5:T(8,128)S(1)} %convolution_bitcast_fusion.1, f32[4,8,2,8,216]{4,3,2,1,0:T(8,128)S(1)} %copy-done.2, f32[2,8,216]{2,0,1:T(2,128)S(1)} %copy-done.10, f32[4,8]{1,0:T(4,128)S(1)} %copy-done.33), kind=kLoop, calls=%fused_computation.56 | loop fusion | flops 1299456 | bytes 1451648 | tf_op jit(solution)/shard_map/reduce_sum | solution.py:175
  133.9 0.7 copy.475
  134.6 1.7 %reshape.11733 = f32[4,16,432]{2,0,1:T(4,128)} reshape(f32[4,2,8,2,1,216]{5,3,0,2,1,4:T(2,128)} %copy.475) | data formatting | bytes 221184 | tf_op jit(solution)/shard_map/mul | solution.py:175
  136.3 4.4 %all-to-all-start.5 = ((f32[4,16,432]{2,0,1:T(4,128)}), f32[4,16,432]{2,0,1:T(4,128)}, u32[]{:S(2)}, u32[]{:S(2)}) async-start(f32[4,16,432]{2,0,1:T(4,128)} %reshape.11733), calls=%async_computation.5 | async-start | bytes 262144 | tf_op jit(solution)/shard_map/all_to_all | solution.py:239
  140.8 0.9 reshape_reshape_reshape_reshape.6
  141.6 1.1 fusion.430
  142.8 2.9 %multiply_subtract_fusion.1 = (f32[8,8,1,8,1,1,216]{6,3,1,4,0,5,2:T(8,128)S(1)}, f32[8,8,1,8,1,1,216]{6,3,1,4,0,5,2:T(8,128)S(1)}) fusion(f32[8,8,8,216]{3,2,1,0:T(8,128)S(1)} %multiply_reduce_fusion.5, f32[8,8,216]{2,1,0:T(8,128)S(1)} %bitcast.579, f32[8,8,216]{2,1,0:T(8,128)} %sqrt.132, f32[8]{0:T(128)S(1)} %copy-done.48, f32[8,8,216]{2,1,0:T(8,128)S(1)} %bitcast.581), kind=kLoop, calls=%fused_computation.67 | loop fusion | flops 995328 | bytes 1493024 | tf_op jit(solution)/shard_map/sub | solution.py:120
  145.7 1.4 convolution_bitcast_fusion.5
  147.8 1.4 all-to-all-done.5
  149.2 1.1 reshape_reshape.8
  150.7 3.5 %convolution_bitcast_fusion = f32[8,8,1,8,2,1,216]{6,1,0,3,5,4,2:T(8,128)S(1)} fusion(f32[8,216,216,1,1]{2,1,3,0,4:T(8,128)} %constant.2448, f32[8,8,1,1,1,216]{5,1,3,0,4,2:T(8,128)S(1)} %get-tuple-element.29, f32[8,8,1,1,1,216]{5,1,3,0,4,2:T(8,128)S(1)} %get-tuple-element.28), kind=kOutput, calls=%fused_computation.8 | convolution fusion | flops 573336576 | bytes 2488320 | tf_op jit(solution)/shard_map/pkbxhs,cqs->pkbcxhq/dot_general | solution.py:171
  154.3 2.7 %subtract_reduce_fusion = (f32[8,8,216]{2,0,1:T(8,128)S(1)}, f32[8,8,216]{2,0,1:T(8,128)S(1)}) fusion(f32[8,8,1,8,2,1,216]{6,1,0,3,5,4,2:T(8,128)S(1)} %convolution_bitcast_fusion, f32[8,8,8,216]{3,2,1,0:T(8,128)S(1)} %multiply_reduce_fusion, f32[8,216]{1,0:T(8,128)S(1)} %copy-done.12, f32[8,8]{1,0:T(8,128)S(1)} %copy-done.16), kind=kLoop, calls=%fused_computation.53 | loop fusion | flops 1299456 | bytes 1444864 | tf_op jit(solution)/shard_map/reduce_sum | solution.py:175
  157.2 0.8 mul.4773
  158.1 2.0 %multiply_subtract_fusion = (f32[1,8,8,8,1,1,216]{6,3,1,4,2,5,0:T(8,128)S(1)}, f32[1,8,8,8,1,1,216]{6,3,1,4,2,5,0:T(8,128)S(1)}) fusion(f32[8,8,8,216]{3,2,1,0:T(8,128)S(1)} %multiply_reduce_fusion.4, f32[8,8,216]{2,0,1:T(8,128)S(1)} %copy.418, f32[8,216]{1,0:T(8,128)S(1)} %copy-done.13, f32[8,8]{1,0:T(8,128)S(1)} %copy-done.15, f32[8,8,216]{2,0,1:T(8,128)S(1)} %copy.414), kind=kLoop, calls=%fused_computation.65 | loop fusion | flops 995328 | bytes 1444864 | tf_op jit(solution)/shard_map/sub | solution.py:120
  160.2 1.4 convolution_bitcast_fusion.4
  162.0 0.8 mul.4599
  (317 shorter events, 34.1 us)
Async XLA Ops:
  0.6 11.4 %copy-start.1 = (f32[8,216,216,1,1]{2,1,4,3,0:T(8,128)S(1)}, f32[8,216,216,1,1]{2,1,4,3,0:T(8,128)}, u32[]{:S(2)}) copy-start(f32[8,216,216,1,1]{2,1,4,3,0:T(8,128)} %constant.2450) | copy-start | bytes 4478980
  0.6 9.8 %copy-start.9 = (f32[4]{0:T(128)S(1)}, f32[4]{0:T(128)}, u32[]{:S(2)}) copy-start(f32[4]{0:T(128)} %param.22) | copy-start | bytes 52
  8.3 5.8 %copy-start.30 = (f32[3]{0:T(128)}, f32[3]{0:T(128)S(1)}, u32[]{:S(2)}) copy-start(f32[3]{0:T(128)S(1)} %get-tuple-element.67) | copy-start | bytes 40
  8.3 53.4 %copy-start.28 = (f32[3]{0:T(128)}, f32[3]{0:T(128)S(1)}, u32[]{:S(2)}) copy-start(f32[3]{0:T(128)S(1)} %get-tuple-element.70) | copy-start | bytes 40
  8.3 62.3 %copy-start.26 = (f32[3]{0:T(128)}, f32[3]{0:T(128)S(1)}, u32[]{:S(2)}) copy-start(f32[3]{0:T(128)S(1)} %get-tuple-element.68) | copy-start | bytes 40
  8.3 65.2 %copy-start.25 = (f32[3]{0:T(128)}, f32[3]{0:T(128)S(1)}, u32[]{:S(2)}) copy-start(f32[3]{0:T(128)S(1)} %get-tuple-element.69) | copy-start | bytes 40
  8.6 5.5 %copy-start.31 = (f32[216]{0:T(256)}, f32[216]{0:T(256)S(1)}, u32[]{:S(2)}) copy-start(f32[216]{0:T(256)S(1)} %sqrt.135) | copy-start | bytes 2596
  22.8 37.7 %copy-start.8 = (f32[8,8,432]{2,1,0:T(8,128)S(1)}, f32[8,8,432]{2,1,0:T(8,128)}, u32[]{:S(2)}) copy-start(f32[8,8,432]{2,1,0:T(8,128)} %param.20) | copy-start | bytes 331780
  27.7 56.6 %all-to-all-start.4 = ((f32[16,2,1,2,432]{4,3,1,2,0:T(2,128)}), f32[16,2,1,2,432]{4,3,1,2,0:T(2,128)S(1)}, u32[]{:S(2)}, u32[]{:S(2)}) async-start(f32[16,2,1,2,432]{4,3,1,2,0:T(2,128)} %copy.440), calls=%async_computation.4 | async-start | bytes 262144 | tf_op jit(solution)/shard_map/all_to_all | solution.py:39
  59.8 4.2 %copy-start = (f32[8,216,216,1,1]{2,1,0,4,3:T(8,128)S(1)}, f32[8,216,216,1,1]{2,1,0,4,3:T(8,128)}, u32[]{:S(2)}) copy-start(f32[8,216,216,1,1]{2,1,0,4,3:T(8,128)} %constant.2446) | copy-start | bytes 4478980
  66.7 12.9 %copy-start.20 = (s32[8,8,1,1,1]{1,0,4,3,2:T(8,128)S(1)}, s32[8,8,1,1,1]{1,0,4,3,2:T(8,128)}, u32[]{:S(2)}) copy-start(s32[8,8,1,1,1]{1,0,4,3,2:T(8,128)} %fusion.298) | copy-start | bytes 772
  66.7 12.9 %copy-start.21 = (s32[8,8,1,1,1]{1,0,4,3,2:T(8,128)S(1)}, s32[8,8,1,1,1]{1,0,4,3,2:T(8,128)}, u32[]{:S(2)}) copy-start(s32[8,8,1,1,1]{1,0,4,3,2:T(8,128)} %fusion.300) | copy-start | bytes 772
  66.8 12.9 %copy-start.22 = (s32[8,8,1,1,1]{1,0,4,3,2:T(8,128)S(1)}, s32[8,8,1,1,1]{1,0,4,3,2:T(8,128)}, u32[]{:S(2)}) copy-start(s32[8,8,1,1,1]{1,0,4,3,2:T(8,128)} %fusion.302) | copy-start | bytes 772
  66.8 12.9 %copy-start.29 = (f32[3]{0:T(128)S(1)}, f32[3]{0:T(128)}, u32[]{:S(2)}) copy-start(f32[3]{0:T(128)} %copy-done.28) | copy-start | bytes 40
  66.8 13.0 %copy-start.17 = (s32[8,8,1,1,1,1]{1,0,5,4,3,2:T(8,128)S(1)}, s32[8,8,1,1,1,1]{1,0,5,4,3,2:T(8,128)}, u32[]{:S(2)}) copy-start(s32[8,8,1,1,1,1]{1,0,5,4,3,2:T(8,128)} %fusion.297) | copy-start | bytes 772
  66.8 13.0 %copy-start.18 = (s32[8,8,1,1,1,1]{1,0,5,4,3,2:T(8,128)S(1)}, s32[8,8,1,1,1,1]{1,0,5,4,3,2:T(8,128)}, u32[]{:S(2)}) copy-start(s32[8,8,1,1,1,1]{1,0,5,4,3,2:T(8,128)} %fusion.299) | copy-start | bytes 772
  66.8 13.0 %copy-start.19 = (s32[8,8,1,1,1,1]{1,0,5,4,3,2:T(8,128)S(1)}, s32[8,8,1,1,1,1]{1,0,5,4,3,2:T(8,128)}, u32[]{:S(2)}) copy-start(s32[8,8,1,1,1,1]{1,0,5,4,3,2:T(8,128)} %fusion.301) | copy-start | bytes 772
  66.8 13.7 %copy-start.37 = (s32[4,8,1,1,1,1]{1,0,5,4,3,2:T(4,128)S(1)}, s32[4,8,1,1,1,1]{1,0,5,4,3,2:T(4,128)}, u32[]{:S(2)}) copy-start(s32[4,8,1,1,1,1]{1,0,5,4,3,2:T(4,128)} %fusion.329) | copy-start | bytes 388
  66.8 13.7 %copy-start.38 = (s32[4,8,1,1,1,1]{1,0,5,4,3,2:T(4,128)S(1)}, s32[4,8,1,1,1,1]{1,0,5,4,3,2:T(4,128)}, u32[]{:S(2)}) copy-start(s32[4,8,1,1,1,1]{1,0,5,4,3,2:T(4,128)} %fusion.331) | copy-start | bytes 388
  66.8 13.7 %copy-start.39 = (s32[4,8,1,1,1,1]{1,0,5,4,3,2:T(4,128)S(1)}, s32[4,8,1,1,1,1]{1,0,5,4,3,2:T(4,128)}, u32[]{:S(2)}) copy-start(s32[4,8,1,1,1,1]{1,0,5,4,3,2:T(4,128)} %fusion.333) | copy-start | bytes 388
  66.8 13.8 %copy-start.34 = (s32[4,8,1,1,1]{1,0,4,3,2:T(4,128)S(1)}, s32[4,8,1,1,1]{1,0,4,3,2:T(4,128)}, u32[]{:S(2)}) copy-start(s32[4,8,1,1,1]{1,0,4,3,2:T(4,128)} %fusion.330) | copy-start | bytes 388
  66.8 13.8 %copy-start.35 = (s32[4,8,1,1,1]{1,0,4,3,2:T(4,128)S(1)}, s32[4,8,1,1,1]{1,0,4,3,2:T(4,128)}, u32[]{:S(2)}) copy-start(s32[4,8,1,1,1]{1,0,4,3,2:T(4,128)} %fusion.332) | copy-start | bytes 388
  66.8 13.8 %copy-start.36 = (s32[4,8,1,1,1]{1,0,4,3,2:T(4,128)S(1)}, s32[4,8,1,1,1]{1,0,4,3,2:T(4,128)}, u32[]{:S(2)}) copy-start(s32[4,8,1,1,1]{1,0,4,3,2:T(4,128)} %fusion.334) | copy-start | bytes 388
  66.8 14.5 %copy-start.14 = (f32[4,8,3]{1,2,0:T(4,128)S(1)}, f32[4,8,3]{1,2,0:T(4,128)}, u32[]{:S(2)}) copy-start(f32[4,8,3]{1,2,0:T(4,128)} %copy.442) | copy-start | bytes 1156
  66.9 15.2 %copy-start.7 = (f32[2,8,216,3]{2,1,3,0:T(8,128)S(1)}, f32[2,8,216,3]{2,1,3,0:T(8,128)}, u32[]{:S(2)}) copy-start(f32[2,8,216,3]{2,1,3,0:T(8,128)} %get-tuple-element.54) | copy-start | bytes 124420
  66.9 15.2 %copy-start.11 = (f32[4,8,3]{2,1,0:T(8,128)S(1)}, f32[4,8,3]{2,1,0:T(8,128)}, u32[]{:S(2)}) copy-start(f32[4,8,3]{2,1,0:T(8,128)} %copy.446) | copy-start | bytes 1156
  68.3 14.8 %copy-start.45 = (s32[1,1,8,1,1]{2,4,3,1,0:T(1,128)S(1)}, s32[1,1,8,1,1]{2,4,3,1,0:T(1,128)}, u32[]{:S(2)}) copy-start(s32[1,1,8,1,1]{2,4,3,1,0:T(1,128)} %get-tuple-element.107) | copy-start | bytes 100
  68.3 14.8 %copy-start.46 = (s32[1,1,8,1,1]{2,4,3,1,0:T(1,128)S(1)}, s32[1,1,8,1,1]{2,4,3,1,0:T(1,128)}, u32[]{:S(2)}) copy-start(s32[1,1,8,1,1]{2,4,3,1,0:T(1,128)} %get-tuple-element.108) | copy-start | bytes 100
  68.3 14.8 %copy-start.47 = (s32[1,1,8,1,1]{2,4,3,1,0:T(1,128)S(1)}, s32[1,1,8,1,1]{2,4,3,1,0:T(1,128)}, u32[]{:S(2)}) copy-start(s32[1,1,8,1,1]{2,4,3,1,0:T(1,128)} %fusion.425) | copy-start | bytes 100
  70.7 9.8 %copy-start.27 = (f32[3]{0:T(128)S(1)}, f32[3]{0:T(128)}, u32[]{:S(2)}) copy-start(f32[3]{0:T(128)} %copy-done.26) | copy-start | bytes 40
  84.3 16.8 %all-to-all-start = ((f32[1,64,432]{2,0,1:T(1,128)}), f32[1,64,432]{2,0,1:T(1,128)}, u32[]{:S(2)}, u32[]{:S(2)}) async-start(f32[1,64,432]{2,0,1:T(1,128)} %mul.4774), calls=%async_computation | async-start | bytes 262144 | tf_op jit(solution)/shard_map/all_to_all | solution.py:219
  104.1 3.9 %copy-start.3 = (f32[8,216,216,1,1,1]{2,1,0,5,4,3:T(8,128)S(1)}, f32[8,216,216,1,1,1]{2,1,0,5,4,3:T(8,128)}, u32[]{:S(2)}) copy-start(f32[8,216,216,1,1,1]{2,1,0,5,4,3:T(8,128)} %constant.2447) | copy-start | bytes 4478980
  108.0 1.4 copy-start.4
  108.0 1.4 copy-start.41
  108.0 1.4 copy-start.42
  109.4 16.6 %copy-start.40 = (f32[4,8]{1,0:T(4,128)S(1)}, f32[4,8]{1,0:T(4,128)}, u32[]{:S(2)}) copy-start(f32[4,8]{1,0:T(4,128)} %get-tuple-element.118) | copy-start | bytes 388
  116.3 14.6 %copy-start.33 = (f32[4,8]{1,0:T(4,128)S(1)}, f32[4,8]{1,0:T(4,128)}, u32[]{:S(2)}) copy-start(f32[4,8]{1,0:T(4,128)} %get-tuple-element.117) | copy-start | bytes 388
  116.3 20.0 %all-to-all-start.2 = ((f32[16,2,2,1,432]{4,2,1,3,0:T(2,128)}), f32[16,2,2,1,432]{4,2,1,3,0:T(2,128)S(1)}, u32[]{:S(2)}, u32[]{:S(2)}) async-start(f32[16,2,2,1,432]{4,2,1,3,0:T(2,128)} %copy.405), calls=%async_computation.2 | async-start | bytes 262144 | tf_op jit(solution)/shard_map/all_to_all | solution.py:39
  126.1 4.9 %copy-start.2 = (f32[4,8,2,8,216]{4,3,2,1,0:T(8,128)S(1)}, f32[4,8,2,8,216]{4,3,2,1,0:T(8,128)}, u32[]{:S(2)}) copy-start(f32[4,8,2,8,216]{4,3,2,1,0:T(8,128)} %multiply_reduce_fusion.1) | copy-start | bytes 1327108
  126.1 4.9 %copy-start.10 = (f32[2,8,216]{2,0,1:T(2,128)S(1)}, f32[2,8,216]{2,0,1:T(2,128)}, u32[]{:S(2)}) copy-start(f32[2,8,216]{2,0,1:T(2,128)} %copy.450) | copy-start | bytes 41476
  130.9 11.8 %copy-start.48 = (f32[8]{0:T(128)S(1)}, f32[8]{0:T(128)}, u32[]{:S(2)}) copy-start(f32[8]{0:T(128)} %broadcast_add_fusion.19) | copy-start | bytes 100
  136.3 12.8 %all-to-all-start.5 = ((f32[4,16,432]{2,0,1:T(4,128)}), f32[4,16,432]{2,0,1:T(4,128)}, u32[]{:S(2)}, u32[]{:S(2)}) async-start(f32[4,16,432]{2,0,1:T(4,128)} %reshape.11733), calls=%async_computation.5 | async-start | bytes 262144 | tf_op jit(solution)/shard_map/all_to_all | solution.py:239
  145.7 1.4 copy-start.44
  145.7 4.7 %copy-start.5 = (f32[8,8,216]{2,1,0:T(8,128)S(1)}, f32[8,8,216]{2,1,0:T(8,128)}, u32[]{:S(2)}) copy-start(f32[8,8,216]{2,1,0:T(8,128)} %get-tuple-element.77) | copy-start | bytes 165892
  145.7 4.7 %copy-start.24 = (f32[8,8]{1,0:T(8,128)S(1)}, f32[8,8]{1,0:T(8,128)}, u32[]{:S(2)}) copy-start(f32[8,8]{1,0:T(8,128)} %get-tuple-element.116) | copy-start | bytes 772
  145.7 4.7 %copy-start.43 = (f32[216]{0:T(256)S(1)}, f32[216]{0:T(256)}, u32[]{:S(2)}) copy-start(f32[216]{0:T(256)} %sqrt.142) | copy-start | bytes 2596
  150.2 4.1 %copy-start.12 = (f32[8,216]{1,0:T(8,128)S(1)}, f32[8,216]{1,0:T(8,128)}, u32[]{:S(2)}) copy-start(f32[8,216]{1,0:T(8,128)} %sqrt.143) | copy-start | bytes 20740
  150.3 4.1 %copy-start.16 = (f32[8,8]{1,0:T(8,128)S(1)}, f32[8,8]{1,0:T(8,128)}, u32[]{:S(2)}) copy-start(f32[8,8]{1,0:T(8,128)} %get-tuple-element.115) | copy-start | bytes 772
  154.3 3.8 %copy-start.13 = (f32[8,216]{1,0:T(8,128)S(1)}, f32[8,216]{1,0:T(8,128)}, u32[]{:S(2)}) copy-start(f32[8,216]{1,0:T(8,128)} %sqrt.134) | copy-start | bytes 20740
  154.3 3.8 %copy-start.15 = (f32[8,8]{1,0:T(8,128)S(1)}, f32[8,8]{1,0:T(8,128)}, u32[]{:S(2)}) copy-start(f32[8,8]{1,0:T(8,128)} %broadcast_add_fusion.9) | copy-start | bytes 772
  160.1 1.4 copy-start.6
  160.2 1.4 copy-start.23
  160.2 1.4 copy-start.32
where the time goes:
time: 164 us; the launch traced here: 163 us
  other arithmetic  62.9 us (38%)
  starting transfers between devices  35.7 us (22%)
  local copies, waits for them, and re-layouts  29.5 us (18%)
  matrix products  16.7 us (10%)
  blocking collectives  7.68 us (5%)
  waiting for transfers between devices  7.42 us (5%)
  between operations  2.96 us (2%)
    all_to_all x2, starting transfers between devices, exchange_in_order(): result = lax.all_to_all(result, axes[k], k, k, tiled=True)  23.1 us
    another operation x38, other arithmetic, box_digits(): return jnp.stack([coord_x, coord_y, coord_z], axis=-1).astype(jnp.float32)  14.1 us
    sub x11, other arithmetic, complex_turn(): real_part * cosine - imag_part * sine_part  13.9 us
    dot_general x4, matrix products, adjoint_level(): jnp.einsum('pkbxhs,cqs->pkbcxhq', stacked, interp, precision=lax.Precisio...  11.2 us
    reduce_sum x4, other arithmetic, adjoint_level(): jnp.sum(back_re, axis=1)  10.8 us
    all_to_all x1, starting transfers between devices, forward_steps(): lax.all_to_all(flatten_pairs(array_now), 'sx', split_axis=1, concat_axis=...  8.18 us
    all_to_all x2, blocking collectives, exchange_in_order(): result = lax.all_to_all(result, axes[k], k, k, tiled=True)  7.68 us
    sqrt x17, local copies, waits for them, and re-layouts, phase_angle(): radius = jnp.sqrt(jnp.sum(points * points, axis=-1))  7.16 us
  transfers between devices with their start and end apart: 4, of which 2 were waited for; matrix products, arithmetic and copies ran while one was open for 38% of the time, Pallas kernels for 0%

commit v1 on v0

v1 whole, which is shorter than its diff:
```python
import functools
import math

import jax
import jax.numpy as jnp
import numpy as np
from jax import lax
from jax.experimental import pallas as pl
from jax.experimental.pallas import tpu as pltpu
from jax.sharding import PartitionSpec as P

ORDER = 6
Q = 216
W = 256
F32 = jnp.float32
BF16 = jnp.bfloat16
PATTERNS = (7, 6, 5, 4)
KORD = (7, 0, 6, 1, 5, 2, 4, 3)
CUT = 2 * Q - 384
SPILL = Q - 128


def cheb_points():
    return np.array([(1.0 - math.cos((2 * i + 1) * math.pi / (2 * ORDER))) / 2.0 for i in range(ORDER)])


def child_table():
    nodes = cheb_points()
    halves = []
    for bit in range(2):
        matrix = np.zeros((ORDER, ORDER))
        for row in range(ORDER):
            where = (nodes[row] + bit) / 2.0
            for col in range(ORDER):
                value = 1.0
                for other in range(ORDER):
                    if other != col:
                        value *= (where - nodes[other]) / (nodes[col] - nodes[other])
                matrix[row, col] = value
        halves.append(matrix)
    return np.stack(
        [np.kron(np.kron(halves[e // 4], halves[e // 2 % 2]), halves[e % 2]) for e in range(8)]
    )


def tables():
    table = np.zeros((8, W, W))
    table[:, :Q, :Q] = child_table() / math.sqrt(8.0)
    forward = table.reshape(8 * W, W).astype(np.float32)
    halves = []
    for whole in (forward, np.ascontiguousarray(forward.T)):
        high = whole.astype(jnp.bfloat16)
        low = (whole - high.astype(np.float32)).astype(jnp.bfloat16)
        halves.append((high, low))
    nodes = cheb_points()
    grid = np.full((8, W), 0.5)
    grid[0, :Q] = np.repeat(nodes, ORDER * ORDER)
    grid[1, :Q] = np.tile(np.repeat(nodes, ORDER), ORDER)
    grid[2, :Q] = np.tile(nodes, ORDER * ORDER)
    return halves, grid.astype(np.float32)


def turn_polynomials():
    x = (np.cos(np.pi * (np.arange(400) + 0.5) / 400) + 1.0) / 8.0
    f = np.sqrt(x)
    s = np.polynomial.chebyshev.Chebyshev.fit(x, np.sin(2 * np.pi * f) / f, 5, domain=[0, 0.25])
    c = np.polynomial.chebyshev.Chebyshev.fit(x, np.cos(2 * np.pi * f), 6, domain=[0, 0.25])
    return [
        [float(v) for v in p.convert(kind=np.polynomial.Polynomial).coef] for p in (s, c)
    ]


SIN, COS = turn_polynomials()


def horner(coefs, z):
    value = jnp.full_like(z, coefs[-1])
    for c in coefs[-2::-1]:
        value = value * z + c
    return value


def cis(turns):
    f = turns - jnp.round(turns)
    z = f * f
    return horner(COS, z), f * horner(SIN, z)


def digit_coords(index, digits):
    out = []
    for bit in (2, 1, 0):
        value = None
        for d in range(digits):
            part = (index >> (3 * d + bit)) & 1
            part = part << d if d else part
            value = part if value is None else value + part
        out.append(value)
    return out


def as_f32(values):
    return [v.astype(F32) for v in values]


def rows8():
    return lax.broadcasted_iota(jnp.int32, (8, W), 0)


def travel_rays(corner, side, grid_ref, med):
    p = [side * (corner[d] + grid_ref[d : d + 1, :]) for d in range(3)]
    r = jnp.sqrt(p[0] * p[0] + p[1] * p[1] + p[2] * p[2])
    return r, [p[d] + med[d + 1] * r for d in range(3)]


def patterns(level, rays):
    step = 1.0 / 2 ** (level + 3)
    x, y, z = (step * v for v in rays)
    a, b = x + y, x - y
    return [cis(a + z), cis(a - z), cis(b + z), cis(b - z)]


def pick(table, row):
    return [(c[row : row + 1, :], s[row : row + 1, :]) for c, s in table]


def split16(first, second):
    whole = jnp.concatenate([first, second], axis=0)
    high = whole.astype(BF16)
    return high, (whole - high.astype(F32)).astype(BF16)


def forward_put(xs_ref, e, re, im, turn):
    cols = slice(e * W, (e + 1) * W)
    for s, (c, sn) in enumerate(turn):
        a, b, d, g = re * c, im * sn, im * c, re * sn
        for base, one, two in ((0, a - b, a + b), (64, d + g, d - g)):
            high, low = split16(one, two)
            row = base + 16 * s
            xs_ref[row : row + 16, cols] = high
            xs_ref[128 + row : 144 + row, cols] = low


def product(x, xh, wh, wl):
    both = jnp.dot(x, wh, preferred_element_type=F32)
    return both[:128] + both[128:] + jnp.dot(xh, wl, preferred_element_type=F32)


def forward_product(xs_ref, wh_ref, wl_ref):
    return product(xs_ref[...], xs_ref[0:128, :], wh_ref[...], wl_ref[...])


def adjoint_put(xs_ref, k, first, second):
    for base, one, two in ((0, first[0], second[0]), (64, first[1], second[1])):
        high, low = split16(one, two)
        row = base + 8 * k
        xs_ref[row : row + 16, :] = high
        xs_ref[128 + row : 144 + row, :] = low


def adjoint_child(xs_ref, wh_ref, wl_ref, e, turn):
    cols = slice(e * W, (e + 1) * W)
    y = product(xs_ref[...], xs_ref[0:128, :], wh_ref[:, cols], wl_ref[:, cols])
    re = im = None
    for k, (c, sn) in zip(PATTERNS, turn):
        o = 7 - k
        kr, ki = y[8 * k : 8 * k + 8], y[64 + 8 * k : 72 + 8 * k]
        br, bi = y[8 * o : 8 * o + 8], y[64 + 8 * o : 72 + 8 * o]
        one = c * (kr + br) + sn * (ki - bi)
        two = c * (ki + bi) - sn * (kr - br)
        re, im = (one, two) if re is None else (re + one, im + two)
    return re, im


def quarters(re, im):
    return re[:, :128], re[:, 128:], im[:, :128], im[:, 128:]


def join(a, b):
    return jnp.concatenate([a, b], axis=1)


def unpack(x_ref, tail_ref):
    tail_ref[...] = jnp.zeros_like(tail_ref)
    tail_ref[:, 0:CUT] = x_ref[:, 384 : 2 * Q]
    lane = lax.broadcasted_iota(jnp.int32, (64, 128), 1)
    x0, x1, x2, x3 = x_ref[:, 0:128], x_ref[:, 128:256], x_ref[:, 256:384], tail_ref[...]
    shift = 128 - SPILL
    r1, r2, r3 = (pltpu.roll(v, shift, 1) for v in (x1, x2, x3))
    re = join(x0, jnp.where(lane < SPILL, x1, 0.0))
    im = join(
        jnp.where(lane < shift, r1, r2),
        jnp.where(lane < shift, r2, jnp.where(lane < SPILL, r3, 0.0)),
    )
    return re, im


def pack(parts, out_ref):
    r0, r1, i0, i1 = (parts[64 * c : 64 * c + 64, :] for c in range(4))
    lane = lax.broadcasted_iota(jnp.int32, (64, 128), 1)
    s0, s1 = pltpu.roll(i0, SPILL, 1), pltpu.roll(i1, SPILL, 1)
    out_ref[:, 0:128] = r0
    out_ref[:, 128:256] = jnp.where(lane < SPILL, r1, s0)
    out_ref[:, 256:384] = jnp.where(lane < SPILL, s0, s1)
    out_ref[:, 384 : 2 * Q] = s1[:, 0:CUT]


def medium_of(med_ref):
    return [med_ref[i] for i in range(4)]


def own_source(extra_rows):
    own = lax.axis_index("sy") * 16 + lax.axis_index("sx")
    high = digit_coords(own, 3)
    low = digit_coords(extra_rows, 1)
    return as_f32([low[d] + 2 * high[d] for d in range(3)])


def root_turn(med, corner, rays0):
    r, rays = rays0
    centre = [(v + 0.5) * 0.5 for v in corner]
    travel = med[0] * r
    return cis(travel + centre[0] * rays[0] + centre[1] * rays[1] + centre[2] * rays[2])


def end_turn(med, block, across, grid_ref):
    own = lax.axis_index("sx") * 32 + lax.axis_index("sy")
    high = digit_coords(own, 3)
    row = digit_coords(rows8(), 1)
    fixed = digit_coords(block, 1)
    wr, wf = (1, 2) if across else (2, 1)
    centre = [
        ((4 * high[d] + wf * fixed[d] + wr * row[d]).astype(F32) + 0.5) * (1.0 / 32.0)
        for d in range(3)
    ]
    p = [8.0 * grid_ref[d : d + 1, :] for d in range(3)]
    r = jnp.sqrt(p[0] * p[0] + p[1] * p[1] + p[2] * p[2])
    u = med[0] * r
    for d in range(3):
        u = u + centre[d] * (p[d] + med[d + 1] * r)
    return cis(u)


def level_patterns(level, corner, side, grid_ref, med):
    return patterns(level, travel_rays(corner, side, grid_ref, med)[1])


def level1_tables(grid_ref, med):
    high = digit_coords(lax.axis_index("sy") * 2, 2)
    first = digit_coords(rows8(), 1)
    out = []
    for half in range(2):
        mid = digit_coords(lax.axis_index("sy") * 2 + half, 2)
        corner = as_f32([first[d] + 2 * mid[d] for d in range(3)])
        out.append(level_patterns(1, corner, 1.0, grid_ref, med))
    return out


def level1_turn(both, e):
    upper = rows8() < 4
    return [
        (
            jnp.where(upper, c0[e : e + 1, :], c1[e : e + 1, :]),
            jnp.where(upper, s0[e : e + 1, :], s1[e : e + 1, :]),
        )
        for (c0, s0), (c1, s1) in zip(*both)
    ]


def level2_turn(e, grid_ref, med):
    parent = digit_coords(rows8(), 1)
    child = digit_coords(e, 1)
    corner = as_f32([2 * parent[d] + child[d] for d in range(3)])
    return level_patterns(2, corner, 2.0, grid_ref, med)


def level3_table(grid_ref, med):
    return level_patterns(3, as_f32(digit_coords(rows8(), 1)), 4.0, grid_ref, med)


def rows_of(ref, start, stride, count=8):
    return ref[pl.ds(start, count, stride=stride), :]


def wide(ref, start, stride):
    return join(rows_of(ref, start[0], stride), rows_of(ref, start[1], stride)), join(
        rows_of(ref, start[2], stride), rows_of(ref, start[3], stride)
    )


def forward0(med_ref, grid_ref, x_ref, wh_ref, wl_ref, out_ref, xs_ref, tail_ref):
    med = medium_of(med_ref)
    r, rays = travel_rays(own_source(rows8()), 0.5, grid_ref, med)
    table = patterns(0, rays)
    target = as_f32(digit_coords(rows8(), 1))
    re, im = unpack(x_ref, tail_ref)
    for e in range(8):
        one = slice(e, e + 1)
        c, s = root_turn(med, target, (r[one], [v[one] for v in rays]))
        xr, xi = re[8 * e : 8 * e + 8], im[8 * e : 8 * e + 8]
        forward_put(xs_ref, e, xr * c - xi * s, xr * s + xi * c, pick(table, e))
    y = forward_product(xs_ref, wh_ref, wl_ref)
    for pos, k in enumerate(KORD):
        four = quarters(y[8 * pos : 8 * pos + 8], y[64 + 8 * pos : 72 + 8 * pos])
        for c, v in enumerate(four):
            out_ref[pl.ds((k >> 2) * 16 + c * 4 + (k & 3), 8, stride=32), :] = v


def forward1(chunk, med_ref, grid_ref, x_ref, wh_ref, wl_ref, *rest):
    if chunk == 16:
        other_ref, out_ref, xs_ref = rest
        for dest in range(32):
            out_ref[dest * 16 + 8 : dest * 16 + 16, :] = other_ref[dest * 8 : dest * 8 + 8, :]
    else:
        out_ref, xs_ref = rest
    med = medium_of(med_ref)
    both = level1_tables(grid_ref, med)
    upper = lax.broadcasted_iota(jnp.int32, (8, 128), 0) < 4
    for e in range(8):
        halves = []
        for part in range(2):
            t0 = x_ref[e * 16 + 8 * part : e * 16 + 8 * part + 8, :]
            t1 = x_ref[128 + e * 16 + 8 * part : 128 + e * 16 + 8 * part + 8, :]
            halves.append(
                join(
                    jnp.where(upper, t0, pltpu.roll(t1, 4, 0)),
                    jnp.where(upper, pltpu.roll(t0, 4, 0), t1),
                )
            )
        forward_put(xs_ref, e, halves[0], halves[1], level1_turn(both, e))
    y = forward_product(xs_ref, wh_ref, wl_ref)
    for pos, k in enumerate(KORD):
        four = quarters(y[8 * pos : 8 * pos + 8], y[64 + 8 * pos : 72 + 8 * pos])
        for c, v in enumerate(four):
            for p in range(2):
                start = k * chunk + p * 4 + c
                out_ref[pl.ds(start, 4, stride=8 * chunk), :] = v[4 * p : 4 * p + 4]


def forward23(chunk, med_ref, grid_ref, x_ref, wh_ref, wl_ref, out_ref, xs_ref, mid_ref):
    med = medium_of(med_ref)
    for e in range(8):
        base = (e >> 1) * chunk + (e & 1) * 4
        re, im = wide(x_ref, [base + c for c in range(4)], 4 * chunk)
        forward_put(xs_ref, e, re, im, level2_turn(e, grid_ref, med))
    y = forward_product(xs_ref, wh_ref, wl_ref)
    for pos, k in enumerate(KORD):
        four = quarters(y[8 * pos : 8 * pos + 8], y[64 + 8 * pos : 72 + 8 * pos])
        for c, v in enumerate(four):
            mid_ref[64 * c + 8 * k : 64 * c + 8 * k + 8, :] = v
    table = level3_table(grid_ref, med)
    for e in range(8):
        re, im = wide(mid_ref, [64 * c + e for c in range(4)], 8)
        forward_put(xs_ref, e, re, im, pick(table, e))
    y = forward_product(xs_ref, wh_ref, wl_ref)
    for pos, k in enumerate(KORD):
        c, s = end_turn(med, k, False, grid_ref)
        re, im = y[8 * pos : 8 * pos + 8], y[64 + 8 * pos : 72 + 8 * pos]
        four = quarters(re * c + im * s, im * c - re * s)
        for q, v in enumerate(four):
            mid_ref[pl.ds(64 * q + k, 8, stride=8), :] = v
    pack(mid_ref, out_ref)


def adjoint32(med_ref, grid_ref, x_ref, wh_ref, wl_ref, out_ref, xs_ref, mid_ref, tail_ref):
    med = medium_of(med_ref)
    re, im = unpack(x_ref, tail_ref)
    for k in range(8):
        c, s = end_turn(med, k, True, grid_ref)
        xr, xi = re[8 * k : 8 * k + 8], im[8 * k : 8 * k + 8]
        for q, v in enumerate(quarters(xr * c - xi * s, xr * s + xi * c)):
            mid_ref[64 * q + 8 * k : 64 * q + 8 * k + 8, :] = v
    for k in range(0, 8, 2):
        adjoint_put(
            xs_ref,
            k,
            wide(mid_ref, [64 * c + k for c in range(4)], 8),
            wide(mid_ref, [64 * c + k + 1 for c in range(4)], 8),
        )
    table = level3_table(grid_ref, med)
    for e in range(8):
        re, im = adjoint_child(xs_ref, wh_ref, wl_ref, e, pick(table, e))
        for q, v in enumerate(quarters(re, im)):
            mid_ref[pl.ds(64 * q + e, 8, stride=8), :] = v
    for k in range(0, 8, 2):
        pair = []
        for j in (k, k + 1):
            r0, r1, i0, i1 = (mid_ref[64 * c + 8 * j : 64 * c + 8 * j + 8, :] for c in range(4))
            pair.append((join(r0, r1), join(i0, i1)))
        adjoint_put(xs_ref, k, pair[0], pair[1])
    for e in range(8):
        re, im = adjoint_child(xs_ref, wh_ref, wl_ref, e, level2_turn(e, grid_ref, med))
        for q, v in enumerate(quarters(re, im)):
            out_ref[pl.ds((e >> 1) * 8 + (e & 1) * 4 + q, 8, stride=32), :] = v


def adjoint1(chunk, med_ref, grid_ref, x_ref, wh_ref, wl_ref, out_ref, xs_ref):
    med = medium_of(med_ref)
    both = level1_tables(grid_ref, med)
    for k in range(0, 8, 2):
        pair = []
        for j in (k, k + 1):
            four = []
            for c in range(4):
                start = j * chunk + (chunk - 8) + c
                four.append(
                    jnp.concatenate(
                        [rows_of(x_ref, start + 4 * p, 8 * chunk, 4) for p in range(2)], axis=0
                    )
                )
            pair.append((join(four[0], four[1]), join(four[2], four[3])))
        adjoint_put(xs_ref, k, pair[0], pair[1])
    for e in range(8):
        re, im = adjoint_child(xs_ref, wh_ref, wl_ref, e, level1_turn(both, e))
        for q, v in enumerate(quarters(re, im)):
            for p in range(2):
                start = (8 * p + e) * 16 + 4 * q
                out_ref[start : start + 4, :] = v[4 * p : 4 * p + 4]


def adjoint0(med_ref, grid_ref, x_ref, wh_ref, wl_ref, out_ref, xs_ref, mid_ref):
    med = medium_of(med_ref)
    r, rays = travel_rays(own_source(rows8()), 0.5, grid_ref, med)
    table = patterns(0, rays)
    target = as_f32(digit_coords(rows8(), 1))
    for k in range(0, 8, 2):
        pair = [
            wide(x_ref, [(j >> 2) * 16 + c * 4 + (j & 3) for c in range(4)], 32)
            for j in (k, k + 1)
        ]
        adjoint_put(xs_ref, k, pair[0], pair[1])
    for e in range(8):
        re, im = adjoint_child(xs_ref, wh_ref, wl_ref, e, pick(table, e))
        one = slice(e, e + 1)
        c, s = root_turn(med, target, (r[one], [v[one] for v in rays]))
        for q, v in enumerate(quarters(re * c + im * s, im * c - re * s)):
            mid_ref[pl.ds(64 * q + e, 8, stride=8), :] = v
    pack(mid_ref, out_ref)


def call(kernel, name, out_shape, scratch, levels, *operands):
    vmem = pl.BlockSpec(memory_space=pltpu.VMEM)
    return pl.pallas_call(
        kernel,
        out_shape=jax.ShapeDtypeStruct(out_shape, F32),
        in_specs=[pl.BlockSpec(memory_space=pltpu.SMEM)] + [vmem] * (len(operands) - 1),
        out_specs=vmem,
        scratch_shapes=scratch,
        compiler_params=pltpu.CompilerParams(vmem_limit_bytes=24 * 2**20),
        cost_estimate=pl.CostEstimate(
            flops=levels * 10**9, bytes_accessed=2 * 10**6, transcendentals=0
        ),
        name=name,
    )(*operands)


CHUNK = 16


def shards(forward_weights, adjoint_weights, medium):
    ((fh, fl), (ah, al)), grid = tables()
    fh, fl, ah, al, grid = (jnp.asarray(v) for v in (fh, fl, ah, al, grid))
    fscr = pltpu.VMEM((256, 8 * W), BF16)
    ascr = pltpu.VMEM((256, W), BF16)
    mid = pltpu.VMEM((256, 128), F32)
    tail = pltpu.VMEM((64, 128), F32)
    swap = functools.partial(lax.all_to_all, split_axis=0, concat_axis=0, tiled=True)

    def over(x, axis, count):
        shape = x.shape
        return swap(x.reshape(count, shape[0] // count, 128), axis).reshape(shape)

    fw = forward_weights.reshape(64, 2 * Q)
    f0 = call(forward0, "forward0", (256, 128), [fscr, tail], 1, medium, grid, fw, fh, fl)
    f0 = over(f0, "sx", 16)
    a2 = call(
        adjoint32, "adjoint32", (256, 128), [ascr, mid, tail], 2, medium, grid, adjoint_weights, ah, al
    )
    f1 = functools.partial(forward1, CHUNK)
    both = call(f1, "forward1", (512, 128), [fscr], 1, medium, grid, f0, fh, fl, a2)
    both = over(both, "sy", 32)
    a1 = functools.partial(adjoint1, CHUNK)
    a1 = call(a1, "adjoint1", (256, 128), [ascr], 1, medium, grid, both, ah, al)
    a1 = over(a1, "sx", 16)
    f3 = functools.partial(forward23, CHUNK)
    f3 = call(f3, "forward23", (64, 2 * Q), [fscr, mid], 2, medium, grid, both, fh, fl)
    a0 = call(adjoint0, "adjoint0", (64, 2 * Q), [ascr, mid], 1, medium, grid, a1, ah, al)
    return f3, a0.reshape(8, 8, 2 * Q)


def solution(mesh):
    return jax.shard_map(
        shards,
        mesh=mesh,
        in_specs=(P(("sy", "sx"), None, None), P(("sx", "sy"), None), P()),
        out_specs=(P(("sx", "sy"), None), P(None, ("sy", "sx"), None)),
        check_vma=False,
    )
```

time: 164 us -> 69.2 us (0.42)
  the two profiles are of different devices: /device:TPU:2 before, /device:TPU:8 now
where the time goes in v1:
time: 69.2 us; the launch traced here: 68.7 us
  blocking collectives  25.5 us (37%)
  starting transfers between devices  13.5 us (20%)
  Pallas kernels  12.4 us (18%)
  waiting for transfers between devices  10.1 us (15%)
  local copies, waits for them, and re-layouts  6.5 us (9%)
  between operations  0.71 us (1%)
    all_to_all x1, blocking collectives, over(): return swap(x.reshape(count, shape[0] // count, 128), axis).reshape(shape)  25.5 us
    all_to_all x2, starting transfers between devices, over(): return swap(x.reshape(count, shape[0] // count, 128), axis).reshape(shape)  13.5 us
    pallas_call x6, Pallas kernels, call(): pl.pallas_call(kernel, out_shape=jax.ShapeDtypeStruct(out_shape, F32), in...  12.4 us
    all_to_all x2, waiting for transfers between devices, over(): return swap(x.reshape(count, shape[0] // count, 128), axis).reshape(shape)  10.1 us
    unnamed x22, local copies, waits for them, and re-layouts  6.5 us
  transfers between devices with their start and end apart: 2, of which 2 were waited for; matrix products, arithmetic and copies ran while one was open for 0% of the time, Pallas kernels for 8%

profile of v1, /device:TPU:8, one launch (start us, length us, event | category | flops | bytes accessed | tf_op | source)
XLA Modules:
  0.0 68.7 jit_solution(2891436987135502670)
XLA Ops:
  0.6 0.0 copy-start.10
  0.6 0.0 copy-start.2
  0.7 0.7 copy-done.10
  1.3 0.0 copy-done.2
  1.3 0.0 copy-start
  1.3 0.9 %copy-done = f32[8,8,432]{2,1,0:T(8,128)S(1)} copy-done((f32[8,8,432]{2,1,0:T(8,128)S(1)}, f32[8,8,432]{2,1,0:T(8,128)}, u32[]{:S(2)}) %copy-start) | copy-done | bytes 110616
  2.2 0.0 copy-start.5
  2.2 1.2 %copy-done.5 = bf16[2048,256]{1,0:T(8,128)(2,1)S(1)} copy-done((bf16[2048,256]{1,0:T(8,128)(2,1)S(1)}, bf16[2048,256]{1,0:T(8,128)(2,1)}, u32[]{:S(2)}) %copy-start.5) | copy-done | bytes 1048600
  3.5 0.0 copy-start.7
  3.5 1.2 %copy-done.7 = bf16[2048,256]{1,0:T(8,128)(2,1)S(1)} copy-done((bf16[2048,256]{1,0:T(8,128)(2,1)S(1)}, bf16[2048,256]{1,0:T(8,128)(2,1)}, u32[]{:S(2)}) %copy-start.7) | copy-done | bytes 1048600
  4.7 0.0 copy-start.3
  4.7 0.0 copy-start.4
  4.7 1.9 %forward0.1 = f32[256,128]{1,0:T(8,128)} custom-call(f32[4]{0:T(128)S(1)} %copy-done.2, f32[8,256]{1,0:T(8,128)S(1)} %copy-done.10, f32[64,432]{1,0:T(8,128)S(1)} %bitcast.13, bf16[2048,256]{1,0:T(8,128)(2,1)S(1)} %copy-done.7, bf16[2048,256]{1,0:T(8,128)(2,1)S(1)} %copy-done.5), custom_call_target="tpu_custom_call" | custom-call | flops 1000000000 | bytes 2000000 | tf_op jit(solution)/shard_map/forward0/pallas_call | solution.py:442
  6.6 0.0 copy-start.1
  6.6 9.5 %all-to-all-start = ((f32[16,16,128]{2,1,0:T(8,128)}), f32[16,16,128]{2,1,0:T(8,128)S(1)}, u32[]{:S(2)}, u32[]{:S(2)}) async-start(f32[16,16,128]{2,1,0:T(8,128)} %bitcast.1), calls=%async_computation | async-start | bytes 262144 | tf_op jit(solution)/shard_map/all_to_all | solution.py:470
  16.1 0.0 copy-done.3
  16.1 0.0 copy-done.4
  16.2 0.0 copy-done.1
  16.2 0.0 copy-start.6
  16.2 2.0 %adjoint32.1.rest_0_ = f32[256,128]{1,0:T(8,128)S(1)} custom-call(f32[4]{0:T(128)S(1)} %copy-done.2, f32[8,256]{1,0:T(8,128)S(1)} %copy-done.10, f32[64,432]{1,0:T(8,128)S(1)} %copy-done.1, bf16[256,2048]{1,0:T(8,128)(2,1)S(1)} %copy-done.4, bf16[256,2048]{1,0:T(8,128)(2,1)S(1)} %copy-done.3), custom_call_target="tpu_custom_call" | custom-call | flops 2000000000 | bytes 2000000 | tf_op jit(solution)/shard_map/adjoint32/pallas_call | solution.py:442
  18.2 6.0 %all-to-all-done = f32[16,16,128]{2,1,0:T(8,128)S(1)} async-done(((f32[16,16,128]{2,1,0:T(8,128)}), f32[16,16,128]{2,1,0:T(8,128)S(1)}, u32[]{:S(2)}, u32[]{:S(2)}) %all-to-all-start) | async-done | bytes 131104 | tf_op jit(solution)/shard_map/all_to_all | solution.py:470
  24.2 0.0 copy-done.6
  24.2 0.0 copy-start.8
  24.2 1.2 %copy-done.8 = bf16[2048,256]{1,0:T(8,128)(2,1)S(1)} copy-done((bf16[2048,256]{1,0:T(8,128)(2,1)S(1)}, bf16[2048,256]{1,0:T(8,128)(2,1)}, u32[]{:S(2)}) %copy-start.8) | copy-done | bytes 1048600
  25.5 1.3 %forward1.1 = f32[512,128]{1,0:T(8,128)S(1)} custom-call(f32[4]{0:T(128)S(1)} %copy-done.2, f32[8,256]{1,0:T(8,128)S(1)} %copy-done.10, f32[256,128]{1,0:T(8,128)S(1)} %bitcast.12, bf16[2048,256]{1,0:T(8,128)(2,1)S(1)} %copy-done.8, bf16[2048,256]{1,0:T(8,128)(2,1)S(1)} %copy-done.6, f32[256,128]{1,0:T(8,128)S(1)} %adjoint32.1.rest_0_), custom_call_target="tpu_custom_call" | custom-call | flops 1000000000 | bytes 2000000 | tf_op jit(solution)/shard_map/forward1/pallas_call | solution.py:442
  26.8 25.5 %all_to_all.15 = f32[32,16,128]{2,1,0:T(8,128)S(1)} all-to-all(f32[32,16,128]{2,1,0:T(8,128)S(1)} %bitcast.10), channel_id=1, replica_groups=mesh['sx'=16,'sy'=32] {'sy'}, dimensions={0} | all-to-all | bytes 524288 | tf_op jit(solution)/shard_map/all_to_all | solution.py:470
  52.2 1.9 %adjoint1.1 = f32[256,128]{1,0:T(8,128)} custom-call(f32[4]{0:T(128)S(1)} %copy-done.2, f32[8,256]{1,0:T(8,128)S(1)} %copy-done.10, f32[512,128]{1,0:T(8,128)S(1)} %bitcast.8, bf16[256,2048]{1,0:T(8,128)(2,1)S(1)} %copy-done.4, bf16[256,2048]{1,0:T(8,128)(2,1)S(1)} %copy-done.3), custom_call_target="tpu_custom_call" | custom-call | flops 1000000000 | bytes 2000000 | tf_op jit(solution)/shard_map/adjoint1/pallas_call | solution.py:442
  54.1 4.0 %all-to-all-start.2 = ((f32[16,16,128]{2,1,0:T(8,128)}), f32[16,16,128]{2,1,0:T(8,128)S(1)}, u32[]{:S(2)}, u32[]{:S(2)}) async-start(f32[16,16,128]{2,1,0:T(8,128)} %bitcast.5), calls=%async_computation.2 | async-start | bytes 262144 | tf_op jit(solution)/shard_map/all_to_all | solution.py:470
  58.1 0.0 copy-start.9
  58.1 1.2 %copy-done.9 = bf16[2048,256]{1,0:T(8,128)(2,1)S(1)} copy-done((bf16[2048,256]{1,0:T(8,128)(2,1)S(1)}, bf16[2048,256]{1,0:T(8,128)(2,1)}, u32[]{:S(2)}) %copy-start.9) | copy-done | bytes 1048600
  59.3 3.2 %forward23.1 = f32[64,432]{1,0:T(8,128)} custom-call(f32[4]{0:T(128)S(1)} %copy-done.2, f32[8,256]{1,0:T(8,128)S(1)} %copy-done.10, f32[512,128]{1,0:T(8,128)S(1)} %bitcast.9, bf16[2048,256]{1,0:T(8,128)(2,1)S(1)} %copy-done.9, bf16[2048,256]{1,0:T(8,128)(2,1)S(1)} %copy-done.6), custom_call_target="tpu_custom_call" | custom-call | flops 2000000000 | bytes 2000000 | tf_op jit(solution)/shard_map/forward23/pallas_call | solution.py:442
  62.6 4.1 %all-to-all-done.2 = f32[16,16,128]{2,1,0:T(8,128)S(1)} async-done(((f32[16,16,128]{2,1,0:T(8,128)}), f32[16,16,128]{2,1,0:T(8,128)S(1)}, u32[]{:S(2)}, u32[]{:S(2)}) %all-to-all-start.2) | async-done | bytes 131104 | tf_op jit(solution)/shard_map/all_to_all | solution.py:470
  66.7 2.0 %adjoint0.1 = f32[64,432]{1,0:T(8,128)} custom-call(f32[4]{0:T(128)S(1)} %copy-done.2, f32[8,256]{1,0:T(8,128)S(1)} %copy-done.10, f32[256,128]{1,0:T(8,128)S(1)} %bitcast.11, bf16[256,2048]{1,0:T(8,128)(2,1)S(1)} %copy-done.4, bf16[256,2048]{1,0:T(8,128)(2,1)S(1)} %copy-done.3), custom_call_target="tpu_custom_call" | custom-call | flops 1000000000 | bytes 2000000 | tf_op jit(solution)/shard_map/adjoint0/pallas_call | solution.py:442
Async XLA Ops:
  0.6 0.7 %copy-start.10 = (f32[8,256]{1,0:T(8,128)S(1)}, f32[8,256]{1,0:T(8,128)}, u32[]{:S(2)}) copy-start(f32[8,256]{1,0:T(8,128)} %constant.14.clone.grid_ref) | copy-start | bytes 24580
  0.6 0.7 %copy-start.2 = (f32[4]{0:T(128)S(1)}, f32[4]{0:T(128)}, u32[]{:S(2)}) copy-start(f32[4]{0:T(128)} %med_ref.11) | copy-start | bytes 52
  1.3 0.9 %copy-start = (f32[8,8,432]{2,1,0:T(8,128)S(1)}, f32[8,8,432]{2,1,0:T(8,128)}, u32[]{:S(2)}) copy-start(f32[8,8,432]{2,1,0:T(8,128)} %param.8) | copy-start | bytes 331780
  2.2 1.2 %copy-start.5 = (bf16[2048,256]{1,0:T(8,128)(2,1)S(1)}, bf16[2048,256]{1,0:T(8,128)(2,1)}, u32[]{:S(2)}) copy-start(bf16[2048,256]{1,0:T(8,128)(2,1)} %constant.11.clone.wl_ref) | copy-start | bytes 3145732
  3.5 1.2 %copy-start.7 = (bf16[2048,256]{1,0:T(8,128)(2,1)S(1)}, bf16[2048,256]{1,0:T(8,128)(2,1)}, u32[]{:S(2)}) copy-start(bf16[2048,256]{1,0:T(8,128)(2,1)} %constant.10.clone.wh_ref) | copy-start | bytes 3145732
  4.7 11.5 %copy-start.3 = (bf16[256,2048]{1,0:T(8,128)(2,1)S(1)}, bf16[256,2048]{1,0:T(8,128)(2,1)}, u32[]{:S(2)}) copy-start(bf16[256,2048]{1,0:T(8,128)(2,1)} %constant.13.clone.wl_ref) | copy-start | bytes 3145732
  4.7 11.5 %copy-start.4 = (bf16[256,2048]{1,0:T(8,128)(2,1)S(1)}, bf16[256,2048]{1,0:T(8,128)(2,1)}, u32[]{:S(2)}) copy-start(bf16[256,2048]{1,0:T(8,128)(2,1)} %constant.12.clone.wh_ref) | copy-start | bytes 3145732
  6.6 9.5 %copy-start.1 = (f32[64,432]{1,0:T(8,128)S(1)}, f32[64,432]{1,0:T(8,128)}, u32[]{:S(2)}) copy-start(f32[64,432]{1,0:T(8,128)} %x_ref.1) | copy-start | bytes 331780
  6.6 17.6 %all-to-all-start = ((f32[16,16,128]{2,1,0:T(8,128)}), f32[16,16,128]{2,1,0:T(8,128)S(1)}, u32[]{:S(2)}, u32[]{:S(2)}) async-start(f32[16,16,128]{2,1,0:T(8,128)} %bitcast.1), calls=%async_computation | async-start | bytes 262144 | tf_op jit(solution)/shard_map/all_to_all | solution.py:470
  16.2 8.1 %copy-start.6 = (bf16[2048,256]{1,0:T(8,128)(2,1)S(1)}, bf16[2048,256]{1,0:T(8,128)(2,1)}, u32[]{:S(2)}) copy-start(bf16[2048,256]{1,0:T(8,128)(2,1)} %constant.11.clone.wl_ref) | copy-start | bytes 3145732
  24.2 1.2 %copy-start.8 = (bf16[2048,256]{1,0:T(8,128)(2,1)S(1)}, bf16[2048,256]{1,0:T(8,128)(2,1)}, u32[]{:S(2)}) copy-start(bf16[2048,256]{1,0:T(8,128)(2,1)} %constant.10.clone.wh_ref) | copy-start | bytes 3145732
  54.1 12.5 %all-to-all-start.2 = ((f32[16,16,128]{2,1,0:T(8,128)}), f32[16,16,128]{2,1,0:T(8,128)S(1)}, u32[]{:S(2)}, u32[]{:S(2)}) async-start(f32[16,16,128]{2,1,0:T(8,128)} %bitcast.5), calls=%async_computation.2 | async-start | bytes 262144 | tf_op jit(solution)/shard_map/all_to_all | solution.py:470
  58.1 1.2 %copy-start.9 = (bf16[2048,256]{1,0:T(8,128)(2,1)S(1)}, bf16[2048,256]{1,0:T(8,128)(2,1)}, u32[]{:S(2)}) copy-start(bf16[2048,256]{1,0:T(8,128)(2,1)} %constant.10.clone.wh_ref) | copy-start | bytes 3145732

commit v2 on v1

--- a/solution.py
+++ b/solution.py
@@ -16,6 +16,7 @@
 BF16 = jnp.bfloat16
 PATTERNS = (7, 6, 5, 4)
 KORD = (7, 0, 6, 1, 5, 2, 4, 3)
+PIECES = 4
 CUT = 2 * Q - 384
 SPILL = Q - 128
 
@@ -46,18 +47,9 @@
 def tables():
     table = np.zeros((8, W, W))
     table[:, :Q, :Q] = child_table() / math.sqrt(8.0)
-    forward = table.reshape(8 * W, W).astype(np.float32)
-    halves = []
-    for whole in (forward, np.ascontiguousarray(forward.T)):
-        high = whole.astype(jnp.bfloat16)
-        low = (whole - high.astype(np.float32)).astype(jnp.bfloat16)
-        halves.append((high, low))
-    nodes = cheb_points()
-    grid = np.full((8, W), 0.5)
-    grid[0, :Q] = np.repeat(nodes, ORDER * ORDER)
-    grid[1, :Q] = np.tile(np.repeat(nodes, ORDER), ORDER)
-    grid[2, :Q] = np.tile(nodes, ORDER * ORDER)
-    return halves, grid.astype(np.float32)
+    whole = table.reshape(8 * W, W).astype(np.float32)
+    high = whole.astype(jnp.bfloat16)
+    return high, (whole - high.astype(np.float32)).astype(jnp.bfloat16)
 
 
 def turn_polynomials():
@@ -106,8 +98,22 @@
     return lax.broadcasted_iota(jnp.int32, (8, W), 0)
 
 
-def travel_rays(corner, side, grid_ref, med):
-    p = [side * (corner[d] + grid_ref[d : d + 1, :]) for d in range(3)]
+def grid_points():
+    t = lax.broadcasted_iota(jnp.int32, (8, W), 1)
+    i = (t * 7282) >> 18
+    ij = (t * 10923) >> 16
+    nodes = [float(v) for v in cheb_points()]
+    out = []
+    for n in (i, ij - 6 * i, t - 6 * ij):
+        value = jnp.full((8, W), nodes[5], F32)
+        for m in range(4, -1, -1):
+            value = jnp.where(n == m, nodes[m], value)
+        out.append(value)
+    return out
+
+
+def travel_rays(corner, side, grid, med):
+    p = [side * (corner[d] + grid[d]) for d in range(3)]
     r = jnp.sqrt(p[0] * p[0] + p[1] * p[1] + p[2] * p[2])
     return r, [p[d] + med[d + 1] * r for d in range(3)]
 
@@ -140,13 +146,16 @@
             xs_ref[128 + row : 144 + row, cols] = low
 
 
-def product(x, xh, wh, wl):
-    both = jnp.dot(x, wh, preferred_element_type=F32)
-    return both[:128] + both[128:] + jnp.dot(xh, wl, preferred_element_type=F32)
+def product(x, xh, wh, wl, side):
+    dot = functools.partial(
+        lax.dot_general, dimension_numbers=(((1,), (side,)), ((), ())), preferred_element_type=F32
+    )
+    both = dot(x, wh)
+    return both[:128] + both[128:] + dot(xh, wl)
 
 
 def forward_product(xs_ref, wh_ref, wl_ref):
-    return product(xs_ref[...], xs_ref[0:128, :], wh_ref[...], wl_ref[...])
+    return product(xs_ref[...], xs_ref[0:128, :], wh_ref[...], wl_ref[...], 0)
 
 
 def adjoint_put(xs_ref, k, first, second):
@@ -159,7 +168,7 @@
 
 def adjoint_child(xs_ref, wh_ref, wl_ref, e, turn):
     cols = slice(e * W, (e + 1) * W)
-    y = product(xs_ref[...], xs_ref[0:128, :], wh_ref[:, cols], wl_ref[:, cols])
+    y = product(xs_ref[...], xs_ref[0:128, :], wh_ref[cols, :], wl_ref[cols, :], 1)
     re = im = None
     for k, (c, sn) in zip(PATTERNS, turn):
         o = 7 - k
@@ -205,7 +214,7 @@
 
 
 def medium_of(med_ref):
-    return [med_ref[i] for i in range(4)]
+    return [jnp.broadcast_to(med_ref[0:1, i : i + 1], (8, W)) for i in range(4)]
 
 
 def own_source(extra_rows):
@@ -222,7 +231,7 @@
     return cis(travel + centre[0] * rays[0] + centre[1] * rays[1] + centre[2] * rays[2])
 
 
-def end_turn(med, block, across, grid_ref):
+def end_turn(med, block, across, grid):
     own = lax.axis_index("sx") * 32 + lax.axis_index("sy")
     high = digit_coords(own, 3)
     row = digit_coords(rows8(), 1)
@@ -232,7 +241,7 @@
         ((4 * high[d] + wf * fixed[d] + wr * row[d]).astype(F32) + 0.5) * (1.0 / 32.0)
         for d in range(3)
     ]
-    p = [8.0 * grid_ref[d : d + 1, :] for d in range(3)]
+    p = [8.0 * grid[d] for d in range(3)]
     r = jnp.sqrt(p[0] * p[0] + p[1] * p[1] + p[2] * p[2])
     u = med[0] * r
     for d in range(3):
@@ -240,18 +249,18 @@
     return cis(u)
 
 
-def level_patterns(level, corner, side, grid_ref, med):
-    return patterns(level, travel_rays(corner, side, grid_ref, med)[1])
-
-
-def level1_tables(grid_ref, med):
+def level_patterns(level, corner, side, grid, med):
+    return patterns(level, travel_rays(corner, side, grid, med)[1])
+
+
+def level1_tables(grid, med):
     high = digit_coords(lax.axis_index("sy") * 2, 2)
     first = digit_coords(rows8(), 1)
     out = []
     for half in range(2):
         mid = digit_coords(lax.axis_index("sy") * 2 + half, 2)
         corner = as_f32([first[d] + 2 * mid[d] for d in range(3)])
-        out.append(level_patterns(1, corner, 1.0, grid_ref, med))
+        out.append(level_patterns(1, corner, 1.0, grid, med))
     return out
 
 
@@ -266,15 +275,15 @@
     ]
 
 
-def level2_turn(e, grid_ref, med):
+def level2_turn(e, grid, med):
     parent = digit_coords(rows8(), 1)
     child = digit_coords(e, 1)
     corner = as_f32([2 * parent[d] + child[d] for d in range(3)])
-    return level_patterns(2, corner, 2.0, grid_ref, med)
-
-
-def level3_table(grid_ref, med):
-    return level_patterns(3, as_f32(digit_coords(rows8(), 1)), 4.0, grid_ref, med)
+    return level_patterns(2, corner, 2.0, grid, med)
+
+
+def level3_table(grid, med):
+    return level_patterns(3, as_f32(digit_coords(rows8(), 1)), 4.0, grid, med)
 
 
 def rows_of(ref, start, stride, count=8):
@@ -287,17 +296,34 @@
     )
 
 
-def forward0(med_ref, grid_ref, x_ref, wh_ref, wl_ref, out_ref, xs_ref, tail_ref):
-    med = medium_of(med_ref)
-    r, rays = travel_rays(own_source(rows8()), 0.5, grid_ref, med)
+def forward0(med_hbm, x_hbm, wh_hbm, wl_hbm, out_ref, xs_ref, tail_ref, med_ref, x_ref, wh_ref, wl_ref, sems):
+    copies = [
+        pltpu.make_async_copy(med_hbm, med_ref, sems.at[0]),
+        pltpu.make_async_copy(x_hbm, x_ref, sems.at[1]),
+    ]
+    step = 8 * W // PIECES
+    for i, (src, dst) in enumerate(((wh_hbm, wh_ref), (wl_hbm, wl_ref))):
+        for j in range(PIECES):
+            part = pl.ds(step * j, step)
+            copies.append(
+                pltpu.make_async_copy(src.at[part, :], dst.at[part, :], sems.at[2 + PIECES * i + j])
+            )
+    for copy in copies:
+        copy.start()
+    copies[0].wait()
+    med, grid = medium_of(med_ref), grid_points()
+    r, rays = travel_rays(own_source(rows8()), 0.5, grid, med)
     table = patterns(0, rays)
     target = as_f32(digit_coords(rows8(), 1))
+    copies[1].wait()
     re, im = unpack(x_ref, tail_ref)
     for e in range(8):
         one = slice(e, e + 1)
         c, s = root_turn(med, target, (r[one], [v[one] for v in rays]))
         xr, xi = re[8 * e : 8 * e + 8], im[8 * e : 8 * e + 8]
         forward_put(xs_ref, e, xr * c - xi * s, xr * s + xi * c, pick(table, e))
+    for copy in copies[2:]:
+        copy.wait()
     y = forward_product(xs_ref, wh_ref, wl_ref)
     for pos, k in enumerate(KORD):
         four = quarters(y[8 * pos : 8 * pos + 8], y[64 + 8 * pos : 72 + 8 * pos])
@@ -305,15 +331,15 @@
             out_ref[pl.ds((k >> 2) * 16 + c * 4 + (k & 3), 8, stride=32), :] = v
 
 
-def forward1(chunk, med_ref, grid_ref, x_ref, wh_ref, wl_ref, *rest):
+def forward1(chunk, med_ref, x_ref, wh_ref, wl_ref, *rest):
     if chunk == 16:
         other_ref, out_ref, xs_ref = rest
         for dest in range(32):
             out_ref[dest * 16 + 8 : dest * 16 + 16, :] = other_ref[dest * 8 : dest * 8 + 8, :]
     else:
         out_ref, xs_ref = rest
-    med = medium_of(med_ref)
-    both = level1_tables(grid_ref, med)
+    med, grid = medium_of(med_ref), grid_points()
+    both = level1_tables(grid, med)
     upper = lax.broadcasted_iota(jnp.int32, (8, 128), 0) < 4
     for e in range(8):
         halves = []
@@ -336,24 +362,24 @@
                 out_ref[pl.ds(start, 4, stride=8 * chunk), :] = v[4 * p : 4 * p + 4]
 
 
-def forward23(chunk, med_ref, grid_ref, x_ref, wh_ref, wl_ref, out_ref, xs_ref, mid_ref):
-    med = medium_of(med_ref)
+def forward23(chunk, med_ref, x_ref, wh_ref, wl_ref, out_ref, xs_ref, mid_ref):
+    med, grid = medium_of(med_ref), grid_points()
     for e in range(8):
         base = (e >> 1) * chunk + (e & 1) * 4
         re, im = wide(x_ref, [base + c for c in range(4)], 4 * chunk)
-        forward_put(xs_ref, e, re, im, level2_turn(e, grid_ref, med))
+        forward_put(xs_ref, e, re, im, level2_turn(e, grid, med))
     y = forward_product(xs_ref, wh_ref, wl_ref)
     for pos, k in enumerate(KORD):
         four = quarters(y[8 * pos : 8 * pos + 8], y[64 + 8 * pos : 72 + 8 * pos])
         for c, v in enumerate(four):
             mid_ref[64 * c + 8 * k : 64 * c + 8 * k + 8, :] = v
-    table = level3_table(grid_ref, med)
+    table = level3_table(grid, med)
     for e in range(8):
         re, im = wide(mid_ref, [64 * c + e for c in range(4)], 8)
         forward_put(xs_ref, e, re, im, pick(table, e))
     y = forward_product(xs_ref, wh_ref, wl_ref)
     for pos, k in enumerate(KORD):
-        c, s = end_turn(med, k, False, grid_ref)
+        c, s = end_turn(med, k, False, grid)
         re, im = y[8 * pos : 8 * pos + 8], y[64 + 8 * pos : 72 + 8 * pos]
         four = quarters(re * c + im * s, im * c - re * s)
         for q, v in enumerate(four):
@@ -361,11 +387,11 @@
     pack(mid_ref, out_ref)
 
 
-def adjoint32(med_ref, grid_ref, x_ref, wh_ref, wl_ref, out_ref, xs_ref, mid_ref, tail_ref):
-    med = medium_of(med_ref)
+def adjoint32(med_ref, x_ref, wh_ref, wl_ref, out_ref, xs_ref, mid_ref, tail_ref):
+    med, grid = medium_of(med_ref), grid_points()
     re, im = unpack(x_ref, tail_ref)
     for k in range(8):
-        c, s = end_turn(med, k, True, grid_ref)
+        c, s = end_turn(med, k, True, grid)
         xr, xi = re[8 * k : 8 * k + 8], im[8 * k : 8 * k + 8]
         for q, v in enumerate(quarters(xr * c - xi * s, xr * s + xi * c)):
             mid_ref[64 * q + 8 * k : 64 * q + 8 * k + 8, :] = v
@@ -376,7 +402,7 @@
             wide(mid_ref, [64 * c + k for c in range(4)], 8),
             wide(mid_ref, [64 * c + k + 1 for c in range(4)], 8),
         )
-    table = level3_table(grid_ref, med)
+    table = level3_table(grid, med)
     for e in range(8):
         re, im = adjoint_child(xs_ref, wh_ref, wl_ref, e, pick(table, e))
         for q, v in enumerate(quarters(re, im)):
@@ -388,14 +414,14 @@
             pair.append((join(r0, r1), join(i0, i1)))
         adjoint_put(xs_ref, k, pair[0], pair[1])
     for e in range(8):
-        re, im = adjoint_child(xs_ref, wh_ref, wl_ref, e, level2_turn(e, grid_ref, med))
+        re, im = adjoint_child(xs_ref, wh_ref, wl_ref, e, level2_turn(e, grid, med))
         for q, v in enumerate(quarters(re, im)):
             out_ref[pl.ds((e >> 1) * 8 + (e & 1) * 4 + q, 8, stride=32), :] = v
 
 
-def adjoint1(chunk, med_ref, grid_ref, x_ref, wh_ref, wl_ref, out_ref, xs_ref):
-    med = medium_of(med_ref)
-    both = level1_tables(grid_ref, med)
+def adjoint1(chunk, med_ref, x_ref, wh_ref, wl_ref, out_ref, xs_ref):
+    med, grid = medium_of(med_ref), grid_points()
+    both = level1_tables(grid, med)
     for k in range(0, 8, 2):
         pair = []
         for j in (k, k + 1):
@@ -417,9 +443,9 @@
                 out_ref[start : start + 4, :] = v[4 * p : 4 * p + 4]
 
 
-def adjoint0(med_ref, grid_ref, x_ref, wh_ref, wl_ref, out_ref, xs_ref, mid_ref):
-    med = medium_of(med_ref)
-    r, rays = travel_rays(own_source(rows8()), 0.5, grid_ref, med)
+def adjoint0(med_ref, x_ref, wh_ref, wl_ref, out_ref, xs_ref, mid_ref):
+    med, grid = medium_of(med_ref), grid_points()
+    r, rays = travel_rays(own_source(rows8()), 0.5, grid, med)
     table = patterns(0, rays)
     target = as_f32(digit_coords(rows8(), 1))
     for k in range(0, 8, 2):
@@ -437,15 +463,14 @@
     pack(mid_ref, out_ref)
 
 
-def call(kernel, name, out_shape, scratch, levels, *operands):
-    vmem = pl.BlockSpec(memory_space=pltpu.VMEM)
+def call(kernel, name, out_shape, scratch, levels, *operands, space=pltpu.VMEM, room=16):
     return pl.pallas_call(
         kernel,
         out_shape=jax.ShapeDtypeStruct(out_shape, F32),
-        in_specs=[pl.BlockSpec(memory_space=pltpu.SMEM)] + [vmem] * (len(operands) - 1),
-        out_specs=vmem,
+        in_specs=[pl.BlockSpec(memory_space=space)] * len(operands),
+        out_specs=pl.BlockSpec(memory_space=pltpu.VMEM),
         scratch_shapes=scratch,
-        compiler_params=pltpu.CompilerParams(vmem_limit_bytes=24 * 2**20),
+        compiler_params=pltpu.CompilerParams(vmem_limit_bytes=room * 2**20),
         cost_estimate=pl.CostEstimate(
             flops=levels * 10**9, bytes_accessed=2 * 10**6, transcendentals=0
         ),
@@ -457,8 +482,8 @@
 
 
 def shards(forward_weights, adjoint_weights, medium):
-    ((fh, fl), (ah, al)), grid = tables()
-    fh, fl, ah, al, grid = (jnp.asarray(v) for v in (fh, fl, ah, al, grid))
+    wh, wl = (jnp.asarray(v) for v in tables())
+    medium = medium.reshape(1, 4)
     fscr = pltpu.VMEM((256, 8 * W), BF16)
     ascr = pltpu.VMEM((256, W), BF16)
     mid = pltpu.VMEM((256, 128), F32)
@@ -470,20 +495,35 @@
         return swap(x.reshape(count, shape[0] // count, 128), axis).reshape(shape)
 
     fw = forward_weights.reshape(64, 2 * Q)
-    f0 = call(forward0, "forward0", (256, 128), [fscr, tail], 1, medium, grid, fw, fh, fl)
+    table = pltpu.VMEM((8 * W, W), BF16)
+    own = [pltpu.VMEM((1, 4), F32), pltpu.VMEM((64, 2 * Q), F32), table, table]
+    own.append(pltpu.SemaphoreType.DMA((2 + 2 * PIECES,)))
+    f0 = call(
+        forward0,
+        "forward0",
+        (256, 128),
+        [fscr, tail] + own,
+        1,
+        medium,
+        fw,
+        wh,
+        wl,
+        space=pltpu.HBM,
+        room=58,
+    )
     f0 = over(f0, "sx", 16)
     a2 = call(
-        adjoint32, "adjoint32", (256, 128), [ascr, mid, tail], 2, medium, grid, adjoint_weights, ah, al
+        adjoint32, "adjoint32", (256, 128), [ascr, mid, tail], 2, medium, adjoint_weights, wh, wl
     )
     f1 = functools.partial(forward1, CHUNK)
-    both = call(f1, "forward1", (512, 128), [fscr], 1, medium, grid, f0, fh, fl, a2)
+    both = call(f1, "forward1", (512, 128), [fscr], 1, medium, f0, wh, wl, a2)
     both = over(both, "sy", 32)
     a1 = functools.partial(adjoint1, CHUNK)
-    a1 = call(a1, "adjoint1", (256, 128), [ascr], 1, medium, grid, both, ah, al)
+    a1 = call(a1, "adjoint1", (256, 128), [ascr], 1, medium, both, wh, wl)
     a1 = over(a1, "sx", 16)
     f3 = functools.partial(forward23, CHUNK)
-    f3 = call(f3, "forward23", (64, 2 * Q), [fscr, mid], 2, medium, grid, both, fh, fl)
-    a0 = call(adjoint0, "adjoint0", (64, 2 * Q), [ascr, mid], 1, medium, grid, a1, ah, al)
+    f3 = call(f3, "forward23", (64, 2 * Q), [fscr, mid], 2, medium, both, wh, wl)
+    a0 = call(adjoint0, "adjoint0", (64, 2 * Q), [ascr, mid], 1, medium, a1, wh, wl)
     return f3, a0.reshape(8, 8, 2 * Q)
 
 

time: 69.2 us -> 63.6 us (0.919)
  local copies, waits for them, and re-layouts: 6.5 us -> 0.03 us
  waiting for transfers between devices: 10.1 us -> 12.1 us
  Pallas kernels: 12.4 us -> 11.5 us
    unnamed x22 -> x8, local copies, waits for them, and re-layouts: 6.5 us -> 0.03 us
    all_to_all x2, waiting for transfers between devices: 10.1 us -> 12.1 us  [over(): return swap(x.reshape(count, shape[0] // count, 128), axis).reshape(shape)]
    pallas_call x6, Pallas kernels: 12.4 us -> 11.5 us  [call(): pl.pallas_call(kernel, out_shape=jax.ShapeDtypeStruct(out_shape, F32), in...]
  transfers between devices with their start and end apart: 2 -> 2, of which waited for: 2 -> 2; matrix products, arithmetic and copies ran while one was open for 0% -> 0% of each run, Pallas kernels for 8% -> 7%
where the time goes in v2:
time: 63.6 us; the launch traced here: 63.3 us
  blocking collectives  25.5 us (40%)
  starting transfers between devices  13.5 us (21%)
  waiting for transfers between devices  12.1 us (19%)
  Pallas kernels  11.5 us (18%)
  between operations  0.71 us (1%)
    all_to_all x1, blocking collectives, over(): return swap(x.reshape(count, shape[0] // count, 128), axis).reshape(shape)  25.5 us
    all_to_all x2, starting transfers between devices, over(): return swap(x.reshape(count, shape[0] // count, 128), axis).reshape(shape)  13.5 us
    all_to_all x2, waiting for transfers between devices, over(): return swap(x.reshape(count, shape[0] // count, 128), axis).reshape(shape)  12.1 us
    pallas_call x6, Pallas kernels, call(): pl.pallas_call(kernel, out_shape=jax.ShapeDtypeStruct(out_shape, F32), in...  11.5 us
  transfers between devices with their start and end apart: 2, of which 2 were waited for; matrix products, arithmetic and copies ran while one was open for 0% of the time, Pallas kernels for 7%

profile of v2, /device:TPU:8, one launch (start us, length us, event | category | flops | bytes accessed | tf_op | source)
XLA Modules:
  0.0 63.3 jit_solution(5352465817065634936)
XLA Ops:
  0.6 0.0 copy-start.2
  0.6 0.0 copy-start.3
  0.7 3.1 %forward0.1 = f32[256,128]{1,0:T(8,128)} custom-call(f32[1,4]{1,0:T(1,128)} %bitcast.14, f32[64,432]{1,0:T(8,128)} %bitcast.21, bf16[2048,256]{1,0:T(8,128)(2,1)} %constant.4.clone.wh_hbm.wh_ref, bf16[2048,256]{1,0:T(8,128)(2,1)} %constant.5.clone.wl_hbm.wl_ref), custom_call_target="tpu_custom_call" | custom-call | flops 1000000000 | bytes 2000000 | tf_op jit(solution)/shard_map/forward0/pallas_call | solution.py:467
  3.8 0.0 copy-start
  3.8 0.0 copy-start.1
  3.8 9.5 %all-to-all-start = ((f32[16,16,128]{2,1,0:T(8,128)}), f32[16,16,128]{2,1,0:T(8,128)S(1)}, u32[]{:S(2)}, u32[]{:S(2)}) async-start(f32[16,16,128]{2,1,0:T(8,128)} %bitcast.20), calls=%async_computation | async-start | bytes 262144 | tf_op jit(solution)/shard_map/all_to_all | solution.py:495
  13.3 0.0 copy-done.2
  13.3 0.0 copy-done.3
  13.3 0.0 copy-done
  13.3 0.0 copy-done.1
  13.3 1.8 %adjoint32.1.rest_0_ = f32[256,128]{1,0:T(8,128)S(1)} custom-call(f32[1,4]{1,0:T(1,128)S(1)} %bitcast.15, f32[64,432]{1,0:T(8,128)S(1)} %copy-done, bf16[2048,256]{1,0:T(8,128)(2,1)S(1)} %copy-done.3, bf16[2048,256]{1,0:T(8,128)(2,1)S(1)} %copy-done.2), custom_call_target="tpu_custom_call" | custom-call | flops 2000000000 | bytes 2000000 | tf_op jit(solution)/shard_map/adjoint32/pallas_call | solution.py:467
  15.1 6.3 %all-to-all-done = f32[16,16,128]{2,1,0:T(8,128)S(1)} async-done(((f32[16,16,128]{2,1,0:T(8,128)}), f32[16,16,128]{2,1,0:T(8,128)S(1)}, u32[]{:S(2)}, u32[]{:S(2)}) %all-to-all-start) | async-done | bytes 131104 | tf_op jit(solution)/shard_map/all_to_all | solution.py:495
  21.4 0.8 %forward1.1 = f32[512,128]{1,0:T(8,128)S(1)} custom-call(f32[1,4]{1,0:T(1,128)S(1)} %bitcast.16, f32[256,128]{1,0:T(8,128)S(1)} %bitcast.13, bf16[2048,256]{1,0:T(8,128)(2,1)S(1)} %copy-done.3, bf16[2048,256]{1,0:T(8,128)(2,1)S(1)} %copy-done.2, f32[256,128]{1,0:T(8,128)S(1)} %adjoint32.1.rest_0_), custom_call_target="tpu_custom_call" | custom-call | flops 1000000000 | bytes 2000000 | tf_op jit(solution)/shard_map/forward1/pallas_call | solution.py:467
  22.2 25.5 %all_to_all.15 = f32[32,16,128]{2,1,0:T(8,128)S(1)} all-to-all(f32[32,16,128]{2,1,0:T(8,128)S(1)} %bitcast.11), channel_id=1, replica_groups=mesh['sx'=16,'sy'=32] {'sy'}, dimensions={0} | all-to-all | bytes 524288 | tf_op jit(solution)/shard_map/all_to_all | solution.py:495
  47.6 1.5 %adjoint1.1 = f32[256,128]{1,0:T(8,128)} custom-call(f32[1,4]{1,0:T(1,128)S(1)} %bitcast.17, f32[512,128]{1,0:T(8,128)S(1)} %bitcast.9, bf16[2048,256]{1,0:T(8,128)(2,1)S(1)} %copy-done.3, bf16[2048,256]{1,0:T(8,128)(2,1)S(1)} %copy-done.2), custom_call_target="tpu_custom_call" | custom-call | flops 1000000000 | bytes 2000000 | tf_op jit(solution)/shard_map/adjoint1/pallas_call | solution.py:467
  49.2 4.0 %all-to-all-start.2 = ((f32[16,16,128]{2,1,0:T(8,128)}), f32[16,16,128]{2,1,0:T(8,128)S(1)}, u32[]{:S(2)}, u32[]{:S(2)}) async-start(f32[16,16,128]{2,1,0:T(8,128)} %bitcast.6), calls=%async_computation.2 | async-start | bytes 262144 | tf_op jit(solution)/shard_map/all_to_all | solution.py:495
  53.1 2.7 %forward23.1 = f32[64,432]{1,0:T(8,128)} custom-call(f32[1,4]{1,0:T(1,128)S(1)} %bitcast.18, f32[512,128]{1,0:T(8,128)S(1)} %bitcast.10, bf16[2048,256]{1,0:T(8,128)(2,1)S(1)} %copy-done.3, bf16[2048,256]{1,0:T(8,128)(2,1)S(1)} %copy-done.2), custom_call_target="tpu_custom_call" | custom-call | flops 2000000000 | bytes 2000000 | tf_op jit(solution)/shard_map/forward23/pallas_call | solution.py:467
  55.8 5.8 %all-to-all-done.2 = f32[16,16,128]{2,1,0:T(8,128)S(1)} async-done(((f32[16,16,128]{2,1,0:T(8,128)}), f32[16,16,128]{2,1,0:T(8,128)S(1)}, u32[]{:S(2)}, u32[]{:S(2)}) %all-to-all-start.2) | async-done | bytes 131104 | tf_op jit(solution)/shard_map/all_to_all | solution.py:495
  61.7 1.6 %adjoint0.1 = f32[64,432]{1,0:T(8,128)} custom-call(f32[1,4]{1,0:T(1,128)S(1)} %bitcast.19, f32[256,128]{1,0:T(8,128)S(1)} %bitcast.12, bf16[2048,256]{1,0:T(8,128)(2,1)S(1)} %copy-done.3, bf16[2048,256]{1,0:T(8,128)(2,1)S(1)} %copy-done.2), custom_call_target="tpu_custom_call" | custom-call | flops 1000000000 | bytes 2000000 | tf_op jit(solution)/shard_map/adjoint0/pallas_call | solution.py:467
Async XLA Ops:
  0.6 12.7 %copy-start.2 = (bf16[2048,256]{1,0:T(8,128)(2,1)S(1)}, bf16[2048,256]{1,0:T(8,128)(2,1)}, u32[]{:S(2)}) copy-start(bf16[2048,256]{1,0:T(8,128)(2,1)} %constant.5.clone.wl_hbm.wl_ref) | copy-start | bytes 3145732
  0.6 12.7 %copy-start.3 = (bf16[2048,256]{1,0:T(8,128)(2,1)S(1)}, bf16[2048,256]{1,0:T(8,128)(2,1)}, u32[]{:S(2)}) copy-start(bf16[2048,256]{1,0:T(8,128)(2,1)} %constant.4.clone.wh_hbm.wh_ref) | copy-start | bytes 3145732
  3.8 9.6 %copy-start = (f32[64,432]{1,0:T(8,128)S(1)}, f32[64,432]{1,0:T(8,128)}, u32[]{:S(2)}) copy-start(f32[64,432]{1,0:T(8,128)} %x_ref.1) | copy-start | bytes 331780
  3.8 9.6 %copy-start.1 = (f32[4]{0:T(128)S(1)}, f32[4]{0:T(128)}, u32[]{:S(2)}) copy-start(f32[4]{0:T(128)} %param.7) | copy-start | bytes 52
  3.8 17.6 %all-to-all-start = ((f32[16,16,128]{2,1,0:T(8,128)}), f32[16,16,128]{2,1,0:T(8,128)S(1)}, u32[]{:S(2)}, u32[]{:S(2)}) async-start(f32[16,16,128]{2,1,0:T(8,128)} %bitcast.20), calls=%async_computation | async-start | bytes 262144 | tf_op jit(solution)/shard_map/all_to_all | solution.py:495
  49.2 12.5 %all-to-all-start.2 = ((f32[16,16,128]{2,1,0:T(8,128)}), f32[16,16,128]{2,1,0:T(8,128)S(1)}, u32[]{:S(2)}, u32[]{:S(2)}) async-start(f32[16,16,128]{2,1,0:T(8,128)} %bitcast.6), calls=%async_computation.2 | async-start | bytes 262144 | tf_op jit(solution)/shard_map/all_to_all | solution.py:495

commit v3 on v2

--- a/solution.py
+++ b/solution.py
@@ -211,6 +211,24 @@
     out_ref[:, 128:256] = jnp.where(lane < SPILL, r1, s0)
     out_ref[:, 256:384] = jnp.where(lane < SPILL, s0, s1)
     out_ref[:, 384 : 2 * Q] = s1[:, 0:CUT]
+
+
+def lanes(shape):
+    return lax.broadcasted_iota(jnp.int32, shape, 1)
+
+
+def spread(t3, rows):
+    own = lanes(rows[0].shape) < SPILL
+    return [
+        jnp.where(own, row, pltpu.roll(t, shift, 1))
+        for row, t, shift in zip(rows, t3, (SPILL, SPILL - 40, SPILL - 80))
+    ]
+
+
+def gather3(rows):
+    a, b, c = (pltpu.roll(v, s, 1) for v, s in zip(rows, (40, 80, 120)))
+    lane = lanes(a.shape)
+    return jnp.where(lane < 40, a, jnp.where(lane < 80, b, c))
 
 
 def medium_of(med_ref):
@@ -315,11 +333,14 @@
     r, rays = travel_rays(own_source(rows8()), 0.5, grid, med)
     table = patterns(0, rays)
     target = as_f32(digit_coords(rows8(), 1))
+    turns = []
+    for e in range(8):
+        one = slice(e, e + 1)
+        turns.append(root_turn(med, target, (r[one], [v[one] for v in rays])))
     copies[1].wait()
     re, im = unpack(x_ref, tail_ref)
     for e in range(8):
-        one = slice(e, e + 1)
-        c, s = root_turn(med, target, (r[one], [v[one] for v in rays]))
+        c, s = turns[e]
         xr, xi = re[8 * e : 8 * e + 8], im[8 * e : 8 * e + 8]
         forward_put(xs_ref, e, xr * c - xi * s, xr * s + xi * c, pick(table, e))
     for copy in copies[2:]:
@@ -331,13 +352,12 @@
             out_ref[pl.ds((k >> 2) * 16 + c * 4 + (k & 3), 8, stride=32), :] = v
 
 
-def forward1(chunk, med_ref, x_ref, wh_ref, wl_ref, *rest):
-    if chunk == 16:
-        other_ref, out_ref, xs_ref = rest
-        for dest in range(32):
-            out_ref[dest * 16 + 8 : dest * 16 + 16, :] = other_ref[dest * 8 : dest * 8 + 8, :]
-    else:
-        out_ref, xs_ref = rest
+def forward1(med_ref, x_ref, wh_ref, wl_ref, other_ref, out_ref, xs_ref):
+    for q in range(7):
+        for group in range(0, 32, 8):
+            out_ref[pl.ds(group * 14 + 7 + q, 8, stride=14), :] = other_ref[
+                q * 32 + group : q * 32 + group + 8, :
+            ]
     med, grid = medium_of(med_ref), grid_points()
     both = level1_tables(grid, med)
     upper = lax.broadcasted_iota(jnp.int32, (8, 128), 0) < 4
@@ -355,19 +375,25 @@
         forward_put(xs_ref, e, halves[0], halves[1], level1_turn(both, e))
     y = forward_product(xs_ref, wh_ref, wl_ref)
     for pos, k in enumerate(KORD):
-        four = quarters(y[8 * pos : 8 * pos + 8], y[64 + 8 * pos : 72 + 8 * pos])
-        for c, v in enumerate(four):
-            for p in range(2):
-                start = k * chunk + p * 4 + c
-                out_ref[pl.ds(start, 4, stride=8 * chunk), :] = v[4 * p : 4 * p + 4]
-
-
-def forward23(chunk, med_ref, x_ref, wh_ref, wl_ref, out_ref, xs_ref, mid_ref):
+        r0, r1, i0, i1 = quarters(y[8 * pos : 8 * pos + 8], y[64 + 8 * pos : 72 + 8 * pos])
+        last = pltpu.roll(i1, 4, 0)
+        u4, u5, u6 = spread((last, last, i1), (r1, i1, r1))
+        low, high = slice(0, 4), slice(4, 8)
+        rows = (r0[low], i0[low], r0[high], i0[high], u4[low], u5[low], u6[high])
+        for q, v in enumerate(rows):
+            out_ref[pl.ds(k * 14 + q, 4, stride=112), :] = v
+
+
+def forward23(med_ref, x_ref, wh_ref, wl_ref, out_ref, xs_ref, mid_ref):
     med, grid = medium_of(med_ref), grid_points()
-    for e in range(8):
-        base = (e >> 1) * chunk + (e & 1) * 4
-        re, im = wide(x_ref, [base + c for c in range(4)], 4 * chunk)
-        forward_put(xs_ref, e, re, im, level2_turn(e, grid, med))
+    for m in range(4):
+        row = [rows_of(x_ref, m * 14 + q, 56) for q in range(7)]
+        pair = (
+            (join(row[0], row[4]), join(row[1], row[5])),
+            (join(row[2], row[6]), join(row[3], gather3(row[4:]))),
+        )
+        for e, (re, im) in zip((2 * m, 2 * m + 1), pair):
+            forward_put(xs_ref, e, re, im, level2_turn(e, grid, med))
     y = forward_product(xs_ref, wh_ref, wl_ref)
     for pos, k in enumerate(KORD):
         four = quarters(y[8 * pos : 8 * pos + 8], y[64 + 8 * pos : 72 + 8 * pos])
@@ -413,26 +439,28 @@
             r0, r1, i0, i1 = (mid_ref[64 * c + 8 * j : 64 * c + 8 * j + 8, :] for c in range(4))
             pair.append((join(r0, r1), join(i0, i1)))
         adjoint_put(xs_ref, k, pair[0], pair[1])
-    for e in range(8):
-        re, im = adjoint_child(xs_ref, wh_ref, wl_ref, e, level2_turn(e, grid, med))
-        for q, v in enumerate(quarters(re, im)):
-            out_ref[pl.ds((e >> 1) * 8 + (e & 1) * 4 + q, 8, stride=32), :] = v
-
-
-def adjoint1(chunk, med_ref, x_ref, wh_ref, wl_ref, out_ref, xs_ref):
+    for m in range(4):
+        first, second = (
+            quarters(*adjoint_child(xs_ref, wh_ref, wl_ref, e, level2_turn(e, grid, med)))
+            for e in (2 * m, 2 * m + 1)
+        )
+        tails = spread((second[3],) * 3, (first[1], first[3], second[1]))
+        for q, v in enumerate((first[0], first[2], second[0], second[2], *tails)):
+            out_ref[pl.ds(q * 32 + m, 8, stride=4), :] = v
+
+
+def adjoint1(med_ref, x_ref, wh_ref, wl_ref, out_ref, xs_ref):
     med, grid = medium_of(med_ref), grid_points()
     both = level1_tables(grid, med)
     for k in range(0, 8, 2):
         pair = []
         for j in (k, k + 1):
-            four = []
-            for c in range(4):
-                start = j * chunk + (chunk - 8) + c
-                four.append(
-                    jnp.concatenate(
-                        [rows_of(x_ref, start + 4 * p, 8 * chunk, 4) for p in range(2)], axis=0
-                    )
-                )
+            row = [rows_of(x_ref, j * 14 + 7 + q, 112, 4) for q in range(7)]
+            t3 = gather3(row[4:])
+            four = [
+                jnp.concatenate(v, axis=0)
+                for v in ((row[0], row[2]), (row[4], row[6]), (row[1], row[3]), (row[5], t3))
+            ]
             pair.append((join(four[0], four[1]), join(four[2], four[3])))
         adjoint_put(xs_ref, k, pair[0], pair[1])
     for e in range(8):
@@ -478,9 +506,6 @@
     )(*operands)
 
 
-CHUNK = 16
-
-
 def shards(forward_weights, adjoint_weights, medium):
     wh, wl = (jnp.asarray(v) for v in tables())
     medium = medium.reshape(1, 4)
@@ -490,9 +515,9 @@
     tail = pltpu.VMEM((64, 128), F32)
     swap = functools.partial(lax.all_to_all, split_axis=0, concat_axis=0, tiled=True)
 
-    def over(x, axis, count):
+    def over(x, axis, count, rows):
         shape = x.shape
-        return swap(x.reshape(count, shape[0] // count, 128), axis).reshape(shape)
+        return swap(x.reshape(count, -1, rows, 128), axis).reshape(shape)
 
     fw = forward_weights.reshape(64, 2 * Q)
     table = pltpu.VMEM((8 * W, W), BF16)
@@ -511,18 +536,15 @@
         space=pltpu.HBM,
         room=58,
     )
-    f0 = over(f0, "sx", 16)
+    f0 = over(f0, "sx", 16, 8)
     a2 = call(
-        adjoint32, "adjoint32", (256, 128), [ascr, mid, tail], 2, medium, adjoint_weights, wh, wl
-    )
-    f1 = functools.partial(forward1, CHUNK)
-    both = call(f1, "forward1", (512, 128), [fscr], 1, medium, f0, wh, wl, a2)
-    both = over(both, "sy", 32)
-    a1 = functools.partial(adjoint1, CHUNK)
-    a1 = call(a1, "adjoint1", (256, 128), [ascr], 1, medium, both, wh, wl)
-    a1 = over(a1, "sx", 16)
-    f3 = functools.partial(forward23, CHUNK)
-    f3 = call(f3, "forward23", (64, 2 * Q), [fscr, mid], 2, medium, both, wh, wl)
+        adjoint32, "adjoint32", (224, 128), [ascr, mid, tail], 2, medium, adjoint_weights, wh, wl
+    )
+    both = call(forward1, "forward1", (448, 128), [fscr], 1, medium, f0, wh, wl, a2)
+    both = over(both, "sy", 32, 2)
+    a1 = call(adjoint1, "adjoint1", (256, 128), [ascr], 1, medium, both, wh, wl)
+    a1 = over(a1, "sx", 16, 8)
+    f3 = call(forward23, "forward23", (64, 2 * Q), [fscr, mid], 2, medium, both, wh, wl)
     a0 = call(adjoint0, "adjoint0", (64, 2 * Q), [ascr, mid], 1, medium, a1, wh, wl)
     return f3, a0.reshape(8, 8, 2 * Q)
 

time: 63.6 us -> 62.9 us (0.989)
  blocking collectives: 25.5 us -> 24.8 us
    all_to_all x1, blocking collectives: 25.5 us -> 24.8 us  [over(): return swap(x.reshape(count, -1, rows, 128), axis).reshape(shape)]
where the time goes in v3:
time: 62.9 us; the launch traced here: 62.6 us
  blocking collectives  24.8 us (39%)
  starting transfers between devices  13.5 us (21%)
  waiting for transfers between devices  12.1 us (19%)
  Pallas kernels  11.5 us (18%)
  between operations  0.71 us (1%)
    all_to_all x1, blocking collectives, over(): return swap(x.reshape(count, -1, rows, 128), axis).reshape(shape)  24.8 us
    all_to_all x2, starting transfers between devices, over(): return swap(x.reshape(count, -1, rows, 128), axis).reshape(shape)  13.5 us
    all_to_all x2, waiting for transfers between devices, over(): return swap(x.reshape(count, -1, rows, 128), axis).reshape(shape)  12.1 us
    pallas_call x6, Pallas kernels, call(): pl.pallas_call(kernel, out_shape=jax.ShapeDtypeStruct(out_shape, F32), in...  11.5 us
  transfers between devices with their start and end apart: 2, of which 2 were waited for; matrix products, arithmetic and copies ran while one was open for 0% of the time, Pallas kernels for 7%

profile of v3, /device:TPU:8, one launch (start us, length us, event | category | flops | bytes accessed | tf_op | source)
XLA Modules:
  0.0 62.6 jit_solution(10686628241651373504)
XLA Ops:
  0.6 0.0 copy-start.2
  0.6 0.0 copy-start.3
  0.7 3.1 %forward0.1 = f32[256,128]{1,0:T(8,128)} custom-call(f32[1,4]{1,0:T(1,128)} %bitcast.14, f32[64,432]{1,0:T(8,128)} %bitcast.21, bf16[2048,256]{1,0:T(8,128)(2,1)} %constant.4.clone.wh_hbm.wh_ref, bf16[2048,256]{1,0:T(8,128)(2,1)} %constant.5.clone.wl_hbm.wl_ref), custom_call_target="tpu_custom_call" | custom-call | flops 1000000000 | bytes 2000000 | tf_op jit(solution)/shard_map/forward0/pallas_call | solution.py:495
  3.8 0.0 copy-start
  3.8 0.0 copy-start.1
  3.8 9.5 %all-to-all-start = ((f32[16,2,8,128]{3,2,1,0:T(8,128)}), f32[16,2,8,128]{3,2,1,0:T(8,128)S(1)}, u32[]{:S(2)}, u32[]{:S(2)}) async-start(f32[16,2,8,128]{3,2,1,0:T(8,128)} %bitcast.20), calls=%async_computation | async-start | bytes 262144 | tf_op jit(solution)/shard_map/all_to_all | solution.py:520
  13.3 0.0 copy-done.2
  13.3 0.0 copy-done.3
  13.3 0.0 copy-done
  13.3 0.0 copy-done.1
  13.3 1.8 %adjoint32.1.other_ref = f32[224,128]{1,0:T(8,128)S(1)} custom-call(f32[1,4]{1,0:T(1,128)S(1)} %bitcast.15, f32[64,432]{1,0:T(8,128)S(1)} %copy-done, bf16[2048,256]{1,0:T(8,128)(2,1)S(1)} %copy-done.3, bf16[2048,256]{1,0:T(8,128)(2,1)S(1)} %copy-done.2), custom_call_target="tpu_custom_call" | custom-call | flops 2000000000 | bytes 2000000 | tf_op jit(solution)/shard_map/adjoint32/pallas_call | solution.py:495
  15.1 6.3 %all-to-all-done = f32[16,2,8,128]{3,2,1,0:T(8,128)S(1)} async-done(((f32[16,2,8,128]{3,2,1,0:T(8,128)}), f32[16,2,8,128]{3,2,1,0:T(8,128)S(1)}, u32[]{:S(2)}, u32[]{:S(2)}) %all-to-all-start) | async-done | bytes 131104 | tf_op jit(solution)/shard_map/all_to_all | solution.py:520
  21.4 0.8 %forward1.1 = f32[448,128]{1,0:T(8,128)S(1)} custom-call(f32[1,4]{1,0:T(1,128)S(1)} %bitcast.16, f32[256,128]{1,0:T(8,128)S(1)} %bitcast.13, bf16[2048,256]{1,0:T(8,128)(2,1)S(1)} %copy-done.3, bf16[2048,256]{1,0:T(8,128)(2,1)S(1)} %copy-done.2, f32[224,128]{1,0:T(8,128)S(1)} %adjoint32.1.other_ref), custom_call_target="tpu_custom_call" | custom-call | flops 1000000000 | bytes 2000000 | tf_op jit(solution)/shard_map/forward1/pallas_call | solution.py:495
  22.2 24.8 %all_to_all.15 = f32[32,7,2,128]{3,2,1,0:T(2,128)S(1)} all-to-all(f32[32,7,2,128]{3,2,1,0:T(2,128)S(1)} %bitcast.11), channel_id=1, replica_groups=mesh['sx'=16,'sy'=32] {'sy'}, dimensions={0} | all-to-all | bytes 458752 | tf_op jit(solution)/shard_map/all_to_all | solution.py:520
  47.0 1.5 %adjoint1.1 = f32[256,128]{1,0:T(8,128)} custom-call(f32[1,4]{1,0:T(1,128)S(1)} %bitcast.17, f32[448,128]{1,0:T(8,128)S(1)} %bitcast.9, bf16[2048,256]{1,0:T(8,128)(2,1)S(1)} %copy-done.3, bf16[2048,256]{1,0:T(8,128)(2,1)S(1)} %copy-done.2), custom_call_target="tpu_custom_call" | custom-call | flops 1000000000 | bytes 2000000 | tf_op jit(solution)/shard_map/adjoint1/pallas_call | solution.py:495
  48.5 4.0 %all-to-all-start.2 = ((f32[16,2,8,128]{3,2,1,0:T(8,128)}), f32[16,2,8,128]{3,2,1,0:T(8,128)S(1)}, u32[]{:S(2)}, u32[]{:S(2)}) async-start(f32[16,2,8,128]{3,2,1,0:T(8,128)} %bitcast.6), calls=%async_computation.2 | async-start | bytes 262144 | tf_op jit(solution)/shard_map/all_to_all | solution.py:520
  52.5 2.7 %forward23.1 = f32[64,432]{1,0:T(8,128)} custom-call(f32[1,4]{1,0:T(1,128)S(1)} %bitcast.18, f32[448,128]{1,0:T(8,128)S(1)} %bitcast.10, bf16[2048,256]{1,0:T(8,128)(2,1)S(1)} %copy-done.3, bf16[2048,256]{1,0:T(8,128)(2,1)S(1)} %copy-done.2), custom_call_target="tpu_custom_call" | custom-call | flops 2000000000 | bytes 2000000 | tf_op jit(solution)/shard_map/forward23/pallas_call | solution.py:495
  55.2 5.8 %all-to-all-done.2 = f32[16,2,8,128]{3,2,1,0:T(8,128)S(1)} async-done(((f32[16,2,8,128]{3,2,1,0:T(8,128)}), f32[16,2,8,128]{3,2,1,0:T(8,128)S(1)}, u32[]{:S(2)}, u32[]{:S(2)}) %all-to-all-start.2) | async-done | bytes 131104 | tf_op jit(solution)/shard_map/all_to_all | solution.py:520
  61.0 1.6 %adjoint0.1 = f32[64,432]{1,0:T(8,128)} custom-call(f32[1,4]{1,0:T(1,128)S(1)} %bitcast.19, f32[256,128]{1,0:T(8,128)S(1)} %bitcast.12, bf16[2048,256]{1,0:T(8,128)(2,1)S(1)} %copy-done.3, bf16[2048,256]{1,0:T(8,128)(2,1)S(1)} %copy-done.2), custom_call_target="tpu_custom_call" | custom-call | flops 1000000000 | bytes 2000000 | tf_op jit(solution)/shard_map/adjoint0/pallas_call | solution.py:495
Async XLA Ops:
  0.6 12.7 %copy-start.2 = (bf16[2048,256]{1,0:T(8,128)(2,1)S(1)}, bf16[2048,256]{1,0:T(8,128)(2,1)}, u32[]{:S(2)}) copy-start(bf16[2048,256]{1,0:T(8,128)(2,1)} %constant.5.clone.wl_hbm.wl_ref) | copy-start | bytes 3145732
  0.6 12.7 %copy-start.3 = (bf16[2048,256]{1,0:T(8,128)(2,1)S(1)}, bf16[2048,256]{1,0:T(8,128)(2,1)}, u32[]{:S(2)}) copy-start(bf16[2048,256]{1,0:T(8,128)(2,1)} %constant.4.clone.wh_hbm.wh_ref) | copy-start | bytes 3145732
  3.8 9.6 %copy-start = (f32[64,432]{1,0:T(8,128)S(1)}, f32[64,432]{1,0:T(8,128)}, u32[]{:S(2)}) copy-start(f32[64,432]{1,0:T(8,128)} %x_ref.1) | copy-start | bytes 331780
  3.8 9.6 %copy-start.1 = (f32[4]{0:T(128)S(1)}, f32[4]{0:T(128)}, u32[]{:S(2)}) copy-start(f32[4]{0:T(128)} %param.7) | copy-start | bytes 52
  3.8 17.6 %all-to-all-start = ((f32[16,2,8,128]{3,2,1,0:T(8,128)}), f32[16,2,8,128]{3,2,1,0:T(8,128)S(1)}, u32[]{:S(2)}, u32[]{:S(2)}) async-start(f32[16,2,8,128]{3,2,1,0:T(8,128)} %bitcast.20), calls=%async_computation | async-start | bytes 262144 | tf_op jit(solution)/shard_map/all_to_all | solution.py:520
  48.5 12.5 %all-to-all-start.2 = ((f32[16,2,8,128]{3,2,1,0:T(8,128)}), f32[16,2,8,128]{3,2,1,0:T(8,128)S(1)}, u32[]{:S(2)}, u32[]{:S(2)}) async-start(f32[16,2,8,128]{3,2,1,0:T(8,128)} %bitcast.6), calls=%async_computation.2 | async-start | bytes 262144 | tf_op jit(solution)/shard_map/all_to_all | solution.py:520

commit v4 on v3

--- a/solution.py
+++ b/solution.py
@@ -16,7 +16,6 @@
 BF16 = jnp.bfloat16
 PATTERNS = (7, 6, 5, 4)
 KORD = (7, 0, 6, 1, 5, 2, 4, 3)
-PIECES = 4
 CUT = 2 * Q - 384
 SPILL = Q - 128
 
@@ -25,7 +24,7 @@
     return np.array([(1.0 - math.cos((2 * i + 1) * math.pi / (2 * ORDER))) / 2.0 for i in range(ORDER)])
 
 
-def child_table():
+def child_halves():
     nodes = cheb_points()
     halves = []
     for bit in range(2):
@@ -39,6 +38,11 @@
                         value *= (where - nodes[other]) / (nodes[col] - nodes[other])
                 matrix[row, col] = value
         halves.append(matrix)
+    return halves
+
+
+def child_table():
+    halves = child_halves()
     return np.stack(
         [np.kron(np.kron(halves[e // 4], halves[e // 2 % 2]), halves[e % 2]) for e in range(8)]
     )
@@ -98,13 +102,59 @@
     return lax.broadcasted_iota(jnp.int32, (8, W), 0)
 
 
+def point_digits(t):
+    i = (t * 7282) >> 18
+    ij = (t * 10923) >> 16
+    return i, ij - 6 * i, t - 6 * ij
+
+
+def build_tables(wh_ref, wl_ref):
+    lane = lax.broadcasted_iota(jnp.int32, (W, 128), 1)
+    wanted = jnp.where(lane < 24, lane & 7, 8)
+    picks = [
+        jnp.where(n == wanted, 1.0, 0.0).astype(BF16)
+        for n in point_digits(lax.broadcasted_iota(jnp.int32, (W, 128), 0))
+    ]
+    digits = point_digits(lax.broadcasted_iota(jnp.int32, (8, W), 1))
+    row = rows8()
+    factors = [[], [], []]
+    for half in child_halves():
+        rest = half / math.sqrt(2.0)
+        pieces = [[], [], []]
+        for _ in range(3):
+            piece = rest.astype(jnp.bfloat16).astype(np.float64)
+            rest = rest - piece
+            columns = []
+            for i in range(ORDER):
+                column = jnp.zeros((8, W), F32)
+                for m in range(ORDER):
+                    column = jnp.where(row == m, float(piece[m, i]), column)
+                columns.append(column)
+            for d in range(3):
+                value = jnp.zeros((8, W), F32)
+                for i in range(ORDER):
+                    value = jnp.where(digits[d] == i, columns[i], value)
+                pieces[d].append(value)
+        for d in range(3):
+            spread_rows = jnp.concatenate(pieces[d] + [jnp.zeros((104, W), F32)], axis=0)
+            factors[d].append(
+                jnp.dot(picks[d], spread_rows.astype(BF16), preferred_element_type=F32)
+            )
+    for yz in range(4):
+        part = factors[1][yz >> 1] * factors[2][yz & 1]
+        for x in range(2):
+            whole = factors[0][x] * part
+            high = whole.astype(BF16)
+            rows = slice((4 * x + yz) * W, (4 * x + yz + 1) * W)
+            wh_ref[rows, :] = high
+            wl_ref[rows, :] = (whole - high.astype(F32)).astype(BF16)
+
+
 def grid_points():
     t = lax.broadcasted_iota(jnp.int32, (8, W), 1)
-    i = (t * 7282) >> 18
-    ij = (t * 10923) >> 16
     nodes = [float(v) for v in cheb_points()]
     out = []
-    for n in (i, ij - 6 * i, t - 6 * ij):
+    for n in point_digits(t):
         value = jnp.full((8, W), nodes[5], F32)
         for m in range(4, -1, -1):
             value = jnp.where(n == m, nodes[m], value)
@@ -304,6 +354,16 @@
     return level_patterns(3, as_f32(digit_coords(rows8(), 1)), 4.0, grid, med)
 
 
+def keep(ref, slot, turn):
+    for i, value in enumerate(v for pair in turn for v in pair):
+        ref[8 * (slot + i) : 8 * (slot + i) + 8, :] = value
+
+
+def kept(ref, slot, count):
+    rows = [ref[8 * (slot + i) : 8 * (slot + i) + 8, :] for i in range(2 * count)]
+    return list(zip(rows[::2], rows[1::2]))
+
+
 def rows_of(ref, start, stride, count=8):
     return ref[pl.ds(start, count, stride=stride), :]
 
@@ -314,20 +374,14 @@
     )
 
 
-def forward0(med_hbm, x_hbm, wh_hbm, wl_hbm, out_ref, xs_ref, tail_ref, med_ref, x_ref, wh_ref, wl_ref, sems):
+def forward0(med_hbm, x_hbm, out_ref, xs_ref, tail_ref, med_ref, x_ref, wh_ref, wl_ref, sems):
     copies = [
         pltpu.make_async_copy(med_hbm, med_ref, sems.at[0]),
         pltpu.make_async_copy(x_hbm, x_ref, sems.at[1]),
     ]
-    step = 8 * W // PIECES
-    for i, (src, dst) in enumerate(((wh_hbm, wh_ref), (wl_hbm, wl_ref))):
-        for j in range(PIECES):
-            part = pl.ds(step * j, step)
-            copies.append(
-                pltpu.make_async_copy(src.at[part, :], dst.at[part, :], sems.at[2 + PIECES * i + j])
-            )
     for copy in copies:
         copy.start()
+    build_tables(wh_ref, wl_ref)
     copies[0].wait()
     med, grid = medium_of(med_ref), grid_points()
     r, rays = travel_rays(own_source(rows8()), 0.5, grid, med)
@@ -343,8 +397,6 @@
         c, s = turns[e]
         xr, xi = re[8 * e : 8 * e + 8], im[8 * e : 8 * e + 8]
         forward_put(xs_ref, e, xr * c - xi * s, xr * s + xi * c, pick(table, e))
-    for copy in copies[2:]:
-        copy.wait()
     y = forward_product(xs_ref, wh_ref, wl_ref)
     for pos, k in enumerate(KORD):
         four = quarters(y[8 * pos : 8 * pos + 8], y[64 + 8 * pos : 72 + 8 * pos])
@@ -352,14 +404,12 @@
             out_ref[pl.ds((k >> 2) * 16 + c * 4 + (k & 3), 8, stride=32), :] = v
 
 
-def forward1(med_ref, x_ref, wh_ref, wl_ref, other_ref, out_ref, xs_ref):
+def forward1(x_ref, wh_ref, wl_ref, other_ref, turn_ref, out_ref, xs_ref):
     for q in range(7):
         for group in range(0, 32, 8):
             out_ref[pl.ds(group * 14 + 7 + q, 8, stride=14), :] = other_ref[
                 q * 32 + group : q * 32 + group + 8, :
             ]
-    med, grid = medium_of(med_ref), grid_points()
-    both = level1_tables(grid, med)
     upper = lax.broadcasted_iota(jnp.int32, (8, 128), 0) < 4
     for e in range(8):
         halves = []
@@ -372,7 +422,7 @@
                     jnp.where(upper, pltpu.roll(t0, 4, 0), t1),
                 )
             )
-        forward_put(xs_ref, e, halves[0], halves[1], level1_turn(both, e))
+        forward_put(xs_ref, e, halves[0], halves[1], kept(turn_ref, 8 * e, 4))
     y = forward_product(xs_ref, wh_ref, wl_ref)
     for pos, k in enumerate(KORD):
         r0, r1, i0, i1 = quarters(y[8 * pos : 8 * pos + 8], y[64 + 8 * pos : 72 + 8 * pos])
@@ -384,7 +434,7 @@
             out_ref[pl.ds(k * 14 + q, 4, stride=112), :] = v
 
 
-def forward23(med_ref, x_ref, wh_ref, wl_ref, out_ref, xs_ref, mid_ref):
+def forward23(med_ref, x_ref, wh_ref, wl_ref, out_ref, turn_ref, xs_ref, mid_ref):
     med, grid = medium_of(med_ref), grid_points()
     for m in range(4):
         row = [rows_of(x_ref, m * 14 + q, 56) for q in range(7)]
@@ -411,9 +461,15 @@
         for q, v in enumerate(four):
             mid_ref[pl.ds(64 * q + k, 8, stride=8), :] = v
     pack(mid_ref, out_ref)
-
-
-def adjoint32(med_ref, x_ref, wh_ref, wl_ref, out_ref, xs_ref, mid_ref, tail_ref):
+    r, rays = travel_rays(own_source(rows8()), 0.5, grid, med)
+    keep(turn_ref, 0, patterns(0, rays))
+    target = as_f32(digit_coords(rows8(), 1))
+    for e in range(8):
+        one = slice(e, e + 1)
+        keep(turn_ref, 8 + 2 * e, [root_turn(med, target, (r[one], [v[one] for v in rays]))])
+
+
+def adjoint32(med_ref, x_ref, wh_ref, wl_ref, out_ref, turn_ref, xs_ref, mid_ref, tail_ref):
     med, grid = medium_of(med_ref), grid_points()
     re, im = unpack(x_ref, tail_ref)
     for k in range(8):
@@ -447,11 +503,12 @@
         tails = spread((second[3],) * 3, (first[1], first[3], second[1]))
         for q, v in enumerate((first[0], first[2], second[0], second[2], *tails)):
             out_ref[pl.ds(q * 32 + m, 8, stride=4), :] = v
-
-
-def adjoint1(med_ref, x_ref, wh_ref, wl_ref, out_ref, xs_ref):
-    med, grid = medium_of(med_ref), grid_points()
     both = level1_tables(grid, med)
+    for e in range(8):
+        keep(turn_ref, 8 * e, level1_turn(both, e))
+
+
+def adjoint1(x_ref, wh_ref, wl_ref, turn_ref, out_ref, xs_ref):
     for k in range(0, 8, 2):
         pair = []
         for j in (k, k + 1):
@@ -464,18 +521,15 @@
             pair.append((join(four[0], four[1]), join(four[2], four[3])))
         adjoint_put(xs_ref, k, pair[0], pair[1])
     for e in range(8):
-        re, im = adjoint_child(xs_ref, wh_ref, wl_ref, e, level1_turn(both, e))
+        re, im = adjoint_child(xs_ref, wh_ref, wl_ref, e, kept(turn_ref, 8 * e, 4))
         for q, v in enumerate(quarters(re, im)):
             for p in range(2):
                 start = (8 * p + e) * 16 + 4 * q
                 out_ref[start : start + 4, :] = v[4 * p : 4 * p + 4]
 
 
-def adjoint0(med_ref, x_ref, wh_ref, wl_ref, out_ref, xs_ref, mid_ref):
-    med, grid = medium_of(med_ref), grid_points()
-    r, rays = travel_rays(own_source(rows8()), 0.5, grid, med)
-    table = patterns(0, rays)
-    target = as_f32(digit_coords(rows8(), 1))
+def adjoint0(x_ref, wh_ref, wl_ref, turn_ref, out_ref, xs_ref, mid_ref):
+    table = kept(turn_ref, 0, 4)
     for k in range(0, 8, 2):
         pair = [
             wide(x_ref, [(j >> 2) * 16 + c * 4 + (j & 3) for c in range(4)], 32)
@@ -484,19 +538,21 @@
         adjoint_put(xs_ref, k, pair[0], pair[1])
     for e in range(8):
         re, im = adjoint_child(xs_ref, wh_ref, wl_ref, e, pick(table, e))
-        one = slice(e, e + 1)
-        c, s = root_turn(med, target, (r[one], [v[one] for v in rays]))
+        ((c, s),) = kept(turn_ref, 8 + 2 * e, 1)
         for q, v in enumerate(quarters(re * c + im * s, im * c - re * s)):
             mid_ref[pl.ds(64 * q + e, 8, stride=8), :] = v
     pack(mid_ref, out_ref)
 
 
 def call(kernel, name, out_shape, scratch, levels, *operands, space=pltpu.VMEM, room=16):
+    several = isinstance(out_shape[0], tuple)
+    shapes = [jax.ShapeDtypeStruct(v, F32) for v in (out_shape if several else (out_shape,))]
+    place = pl.BlockSpec(memory_space=pltpu.VMEM)
     return pl.pallas_call(
         kernel,
-        out_shape=jax.ShapeDtypeStruct(out_shape, F32),
+        out_shape=shapes if several else shapes[0],
         in_specs=[pl.BlockSpec(memory_space=space)] * len(operands),
-        out_specs=pl.BlockSpec(memory_space=pltpu.VMEM),
+        out_specs=[place] * len(shapes) if several else place,
         scratch_shapes=scratch,
         compiler_params=pltpu.CompilerParams(vmem_limit_bytes=room * 2**20),
         cost_estimate=pl.CostEstimate(
@@ -522,7 +578,7 @@
     fw = forward_weights.reshape(64, 2 * Q)
     table = pltpu.VMEM((8 * W, W), BF16)
     own = [pltpu.VMEM((1, 4), F32), pltpu.VMEM((64, 2 * Q), F32), table, table]
-    own.append(pltpu.SemaphoreType.DMA((2 + 2 * PIECES,)))
+    own.append(pltpu.SemaphoreType.DMA((2,)))
     f0 = call(
         forward0,
         "forward0",
@@ -531,21 +587,29 @@
         1,
         medium,
         fw,
+        space=pltpu.HBM,
+        room=58,
+    )
+    f0 = over(f0, "sx", 16, 8)
+    a2, turn1 = call(
+        adjoint32,
+        "adjoint32",
+        ((224, 128), (512, W)),
+        [ascr, mid, tail],
+        2,
+        medium,
+        adjoint_weights,
         wh,
         wl,
-        space=pltpu.HBM,
-        room=58,
-    )
-    f0 = over(f0, "sx", 16, 8)
-    a2 = call(
-        adjoint32, "adjoint32", (224, 128), [ascr, mid, tail], 2, medium, adjoint_weights, wh, wl
-    )
-    both = call(forward1, "forward1", (448, 128), [fscr], 1, medium, f0, wh, wl, a2)
+    )
+    both = call(forward1, "forward1", (448, 128), [fscr], 1, f0, wh, wl, a2, turn1)
     both = over(both, "sy", 32, 2)
-    a1 = call(adjoint1, "adjoint1", (256, 128), [ascr], 1, medium, both, wh, wl)
+    a1 = call(adjoint1, "adjoint1", (256, 128), [ascr], 1, both, wh, wl, turn1)
     a1 = over(a1, "sx", 16, 8)
-    f3 = call(forward23, "forward23", (64, 2 * Q), [fscr, mid], 2, medium, both, wh, wl)
-    a0 = call(adjoint0, "adjoint0", (64, 2 * Q), [ascr, mid], 1, medium, a1, wh, wl)
+    f3, turn0 = call(
+        forward23, "forward23", ((64, 2 * Q), (192, W)), [fscr, mid], 2, medium, both, wh, wl
+    )
+    a0 = call(adjoint0, "adjoint0", (64, 2 * Q), [ascr, mid], 1, a1, wh, wl, turn0)
     return f3, a0.reshape(8, 8, 2 * Q)
 
 

time: 62.9 us -> 62.2 us (0.989)
    pallas_call x6, Pallas kernels: 11.5 us -> 10.9 us  [call(): pl.pallas_call(kernel, out_shape=shapes if several else shapes[0], in_spe...]
where the time goes in v4:
time: 62.2 us; the launch traced here: 61.9 us
  blocking collectives  24.8 us (40%)
  starting transfers between devices  13.5 us (22%)
  waiting for transfers between devices  12 us (19%)
  Pallas kernels  10.9 us (18%)
  between operations  0.71 us (1%)
    all_to_all x1, blocking collectives, over(): return swap(x.reshape(count, -1, rows, 128), axis).reshape(shape)  24.8 us
    all_to_all x2, starting transfers between devices, over(): return swap(x.reshape(count, -1, rows, 128), axis).reshape(shape)  13.5 us
    all_to_all x2, waiting for transfers between devices, over(): return swap(x.reshape(count, -1, rows, 128), axis).reshape(shape)  12 us
    pallas_call x6, Pallas kernels, call(): pl.pallas_call(kernel, out_shape=shapes if several else shapes[0], in_spe...  10.9 us
  transfers between devices with their start and end apart: 2, of which 2 were waited for; matrix products, arithmetic and copies ran while one was open for 0% of the time, Pallas kernels for 7%

profile of v4, /device:TPU:8, one launch (start us, length us, event | category | flops | bytes accessed | tf_op | source)
XLA Modules:
  0.0 61.9 jit_solution(13956561779611452279)
XLA Ops:
  0.6 0.0 copy-start.2
  0.6 0.0 copy-start.3
  0.7 2.6 %forward0.1 = f32[256,128]{1,0:T(8,128)} custom-call(f32[1,4]{1,0:T(1,128)} %bitcast.14, f32[64,432]{1,0:T(8,128)} %bitcast.18), custom_call_target="tpu_custom_call" | custom-call | flops 1000000000 | bytes 2000000 | tf_op jit(solution)/shard_map/forward0/pallas_call | solution.py:551
  3.2 0.0 copy-start
  3.2 0.0 copy-start.1
  3.2 9.5 %all-to-all-start = ((f32[16,2,8,128]{3,2,1,0:T(8,128)}), f32[16,2,8,128]{3,2,1,0:T(8,128)S(1)}, u32[]{:S(2)}, u32[]{:S(2)}) async-start(f32[16,2,8,128]{3,2,1,0:T(8,128)} %bitcast.17), calls=%async_computation | async-start | bytes 262144 | tf_op jit(solution)/shard_map/all_to_all | solution.py:576
  12.8 0.0 copy-done.2
  12.8 0.0 copy-done.3
  12.8 0.0 copy-done
  12.8 0.0 copy-done.1
  12.8 1.9 %adjoint32.1 = (f32[224,128]{1,0:T(8,128)S(1)}, f32[512,256]{1,0:T(8,128)S(1)}) custom-call(f32[1,4]{1,0:T(1,128)S(1)} %bitcast.15, f32[64,432]{1,0:T(8,128)S(1)} %copy-done, bf16[2048,256]{1,0:T(8,128)(2,1)S(1)} %copy-done.3, bf16[2048,256]{1,0:T(8,128)(2,1)S(1)} %copy-done.2), custom_call_target="tpu_custom_call" | custom-call | flops 2000000000 | bytes 2000000 | tf_op jit(solution)/shard_map/adjoint32/pallas_call | solution.py:551
  14.7 6.2 %all-to-all-done = f32[16,2,8,128]{3,2,1,0:T(8,128)S(1)} async-done(((f32[16,2,8,128]{3,2,1,0:T(8,128)}), f32[16,2,8,128]{3,2,1,0:T(8,128)S(1)}, u32[]{:S(2)}, u32[]{:S(2)}) %all-to-all-start) | async-done | bytes 131104 | tf_op jit(solution)/shard_map/all_to_all | solution.py:576
  20.8 0.7 %forward1.1 = f32[448,128]{1,0:T(8,128)S(1)} custom-call(f32[256,128]{1,0:T(8,128)S(1)} %bitcast.13, bf16[2048,256]{1,0:T(8,128)(2,1)S(1)} %copy-done.3, bf16[2048,256]{1,0:T(8,128)(2,1)S(1)} %copy-done.2, f32[224,128]{1,0:T(8,128)S(1)} %get-tuple-element.6.other_ref, f32[512,256]{1,0:T(8,128)S(1)} %get-tuple-element.7.turn_ref), custom_call_target="tpu_custom_call" | custom-call | flops 1000000000 | bytes 2000000 | tf_op jit(solution)/shard_map/forward1/pallas_call | solution.py:551
  21.5 24.8 %all_to_all.15 = f32[32,7,2,128]{3,2,1,0:T(2,128)S(1)} all-to-all(f32[32,7,2,128]{3,2,1,0:T(2,128)S(1)} %bitcast.11), channel_id=1, replica_groups=mesh['sx'=16,'sy'=32] {'sy'}, dimensions={0} | all-to-all | bytes 458752 | tf_op jit(solution)/shard_map/all_to_all | solution.py:576
  46.3 1.5 %adjoint1.1 = f32[256,128]{1,0:T(8,128)} custom-call(f32[448,128]{1,0:T(8,128)S(1)} %bitcast.9, bf16[2048,256]{1,0:T(8,128)(2,1)S(1)} %copy-done.3, bf16[2048,256]{1,0:T(8,128)(2,1)S(1)} %copy-done.2, f32[512,256]{1,0:T(8,128)S(1)} %get-tuple-element.7.turn_ref), custom_call_target="tpu_custom_call" | custom-call | flops 1000000000 | bytes 2000000 | tf_op jit(solution)/shard_map/adjoint1/pallas_call | solution.py:551
  47.8 4.0 %all-to-all-start.2 = ((f32[16,2,8,128]{3,2,1,0:T(8,128)}), f32[16,2,8,128]{3,2,1,0:T(8,128)S(1)}, u32[]{:S(2)}, u32[]{:S(2)}) async-start(f32[16,2,8,128]{3,2,1,0:T(8,128)} %bitcast.6), calls=%async_computation.2 | async-start | bytes 262144 | tf_op jit(solution)/shard_map/all_to_all | solution.py:576
  51.7 2.7 %forward23.1 = (f32[64,432]{1,0:T(8,128)}, f32[192,256]{1,0:T(8,128)S(1)}) custom-call(f32[1,4]{1,0:T(1,128)S(1)} %bitcast.16, f32[448,128]{1,0:T(8,128)S(1)} %bitcast.10, bf16[2048,256]{1,0:T(8,128)(2,1)S(1)} %copy-done.3, bf16[2048,256]{1,0:T(8,128)(2,1)S(1)} %copy-done.2), custom_call_target="tpu_custom_call" | custom-call | flops 2000000000 | bytes 2000000 | tf_op jit(solution)/shard_map/forward23/pallas_call | solution.py:551
  54.4 5.9 %all-to-all-done.2 = f32[16,2,8,128]{3,2,1,0:T(8,128)S(1)} async-done(((f32[16,2,8,128]{3,2,1,0:T(8,128)}), f32[16,2,8,128]{3,2,1,0:T(8,128)S(1)}, u32[]{:S(2)}, u32[]{:S(2)}) %all-to-all-start.2) | async-done | bytes 131104 | tf_op jit(solution)/shard_map/all_to_all | solution.py:576
  60.3 1.6 %adjoint0.1 = f32[64,432]{1,0:T(8,128)} custom-call(f32[256,128]{1,0:T(8,128)S(1)} %bitcast.12, bf16[2048,256]{1,0:T(8,128)(2,1)S(1)} %copy-done.3, bf16[2048,256]{1,0:T(8,128)(2,1)S(1)} %copy-done.2, f32[192,256]{1,0:T(8,128)S(1)} %get-tuple-element.9.turn_ref), custom_call_target="tpu_custom_call" | custom-call | flops 1000000000 | bytes 2000000 | tf_op jit(solution)/shard_map/adjoint0/pallas_call | solution.py:551
Async XLA Ops:
  0.6 12.1 %copy-start.2 = (bf16[2048,256]{1,0:T(8,128)(2,1)S(1)}, bf16[2048,256]{1,0:T(8,128)(2,1)}, u32[]{:S(2)}) copy-start(bf16[2048,256]{1,0:T(8,128)(2,1)} %constant.5.clone.wl_ref) | copy-start | bytes 3145732
  0.6 12.1 %copy-start.3 = (bf16[2048,256]{1,0:T(8,128)(2,1)S(1)}, bf16[2048,256]{1,0:T(8,128)(2,1)}, u32[]{:S(2)}) copy-start(bf16[2048,256]{1,0:T(8,128)(2,1)} %constant.4.clone.wh_ref) | copy-start | bytes 3145732
  3.2 9.6 %copy-start = (f32[64,432]{1,0:T(8,128)S(1)}, f32[64,432]{1,0:T(8,128)}, u32[]{:S(2)}) copy-start(f32[64,432]{1,0:T(8,128)} %x_ref.1) | copy-start | bytes 331780
  3.2 9.6 %copy-start.1 = (f32[4]{0:T(128)S(1)}, f32[4]{0:T(128)}, u32[]{:S(2)}) copy-start(f32[4]{0:T(128)} %param.7) | copy-start | bytes 52
  3.2 17.6 %all-to-all-start = ((f32[16,2,8,128]{3,2,1,0:T(8,128)}), f32[16,2,8,128]{3,2,1,0:T(8,128)S(1)}, u32[]{:S(2)}, u32[]{:S(2)}) async-start(f32[16,2,8,128]{3,2,1,0:T(8,128)} %bitcast.17), calls=%async_computation | async-start | bytes 262144 | tf_op jit(solution)/shard_map/all_to_all | solution.py:576
  47.8 12.5 %all-to-all-start.2 = ((f32[16,2,8,128]{3,2,1,0:T(8,128)}), f32[16,2,8,128]{3,2,1,0:T(8,128)S(1)}, u32[]{:S(2)}, u32[]{:S(2)}) async-start(f32[16,2,8,128]{3,2,1,0:T(8,128)} %bitcast.6), calls=%async_computation.2 | async-start | bytes 262144 | tf_op jit(solution)/shard_map/all_to_all | solution.py:576

commit v5 on v4

--- a/solution.py
+++ b/solution.py
@@ -108,7 +108,7 @@
     return i, ij - 6 * i, t - 6 * ij
 
 
-def build_tables(wh_ref, wl_ref):
+def table_factors():
     lane = lax.broadcasted_iota(jnp.int32, (W, 128), 1)
     wanted = jnp.where(lane < 24, lane & 7, 8)
     picks = [
@@ -140,14 +140,21 @@
             factors[d].append(
                 jnp.dot(picks[d], spread_rows.astype(BF16), preferred_element_type=F32)
             )
+    return factors
+
+
+def built_product(factors, xs_ref):
+    total = None
     for yz in range(4):
         part = factors[1][yz >> 1] * factors[2][yz & 1]
         for x in range(2):
             whole = factors[0][x] * part
             high = whole.astype(BF16)
-            rows = slice((4 * x + yz) * W, (4 * x + yz + 1) * W)
-            wh_ref[rows, :] = high
-            wl_ref[rows, :] = (whole - high.astype(F32)).astype(BF16)
+            low = (whole - high.astype(F32)).astype(BF16)
+            cols = slice((4 * x + yz) * W, (4 * x + yz + 1) * W)
+            one = product(xs_ref[:, cols], xs_ref[0:128, cols], high, low, 0)
+            total = one if total is None else total + one
+    return total
 
 
 def grid_points():
@@ -374,14 +381,14 @@
     )
 
 
-def forward0(med_hbm, x_hbm, out_ref, xs_ref, tail_ref, med_ref, x_ref, wh_ref, wl_ref, sems):
+def forward0(med_hbm, x_hbm, out_ref, xs_ref, tail_ref, med_ref, x_ref, sems):
     copies = [
         pltpu.make_async_copy(med_hbm, med_ref, sems.at[0]),
         pltpu.make_async_copy(x_hbm, x_ref, sems.at[1]),
     ]
     for copy in copies:
         copy.start()
-    build_tables(wh_ref, wl_ref)
+    factors = table_factors()
     copies[0].wait()
     med, grid = medium_of(med_ref), grid_points()
     r, rays = travel_rays(own_source(rows8()), 0.5, grid, med)
@@ -397,7 +404,7 @@
         c, s = turns[e]
         xr, xi = re[8 * e : 8 * e + 8], im[8 * e : 8 * e + 8]
         forward_put(xs_ref, e, xr * c - xi * s, xr * s + xi * c, pick(table, e))
-    y = forward_product(xs_ref, wh_ref, wl_ref)
+    y = built_product(factors, xs_ref)
     for pos, k in enumerate(KORD):
         four = quarters(y[8 * pos : 8 * pos + 8], y[64 + 8 * pos : 72 + 8 * pos])
         for c, v in enumerate(four):
@@ -576,8 +583,7 @@
         return swap(x.reshape(count, -1, rows, 128), axis).reshape(shape)
 
     fw = forward_weights.reshape(64, 2 * Q)
-    table = pltpu.VMEM((8 * W, W), BF16)
-    own = [pltpu.VMEM((1, 4), F32), pltpu.VMEM((64, 2 * Q), F32), table, table]
+    own = [pltpu.VMEM((1, 4), F32), pltpu.VMEM((64, 2 * Q), F32)]
     own.append(pltpu.SemaphoreType.DMA((2,)))
     f0 = call(
         forward0,

time: 62.2 us -> 62.3 us (level)
  no operation moved by 1% of the time
where the time goes in v5:
time: 62.3 us; the launch traced here: 62 us
  blocking collectives  24.8 us (40%)
  starting transfers between devices  13.5 us (22%)
  waiting for transfers between devices  12 us (19%)
  Pallas kernels  11 us (18%)
  between operations  0.71 us (1%)
    all_to_all x1, blocking collectives, over(): return swap(x.reshape(count, -1, rows, 128), axis).reshape(shape)  24.8 us
    all_to_all x2, starting transfers between devices, over(): return swap(x.reshape(count, -1, rows, 128), axis).reshape(shape)  13.5 us
    all_to_all x2, waiting for transfers between devices, over(): return swap(x.reshape(count, -1, rows, 128), axis).reshape(shape)  12 us
    pallas_call x6, Pallas kernels, call(): pl.pallas_call(kernel, out_shape=shapes if several else shapes[0], in_spe...  11 us
  transfers between devices with their start and end apart: 2, of which 2 were waited for; matrix products, arithmetic and copies ran while one was open for 0% of the time, Pallas kernels for 7%

profile of v5, /device:TPU:8, one launch (start us, length us, event | category | flops | bytes accessed | tf_op | source)
XLA Modules:
  0.0 62.0 jit_solution(18356682301802591588)
XLA Ops:
  0.6 0.0 copy-start.2
  0.6 0.0 copy-start.3
  0.7 2.7 %forward0.1 = f32[256,128]{1,0:T(8,128)} custom-call(f32[1,4]{1,0:T(1,128)} %bitcast.14, f32[64,432]{1,0:T(8,128)} %bitcast.18), custom_call_target="tpu_custom_call" | custom-call | flops 1000000000 | bytes 2000000 | tf_op jit(solution)/shard_map/forward0/pallas_call | solution.py:558
  3.4 0.0 copy-start
  3.4 0.0 copy-start.1
  3.4 9.5 %all-to-all-start = ((f32[16,2,8,128]{3,2,1,0:T(8,128)}), f32[16,2,8,128]{3,2,1,0:T(8,128)S(1)}, u32[]{:S(2)}, u32[]{:S(2)}) async-start(f32[16,2,8,128]{3,2,1,0:T(8,128)} %bitcast.17), calls=%async_computation | async-start | bytes 262144 | tf_op jit(solution)/shard_map/all_to_all | solution.py:583
  12.9 0.0 copy-done.2
  12.9 0.0 copy-done.3
  12.9 0.0 copy-done
  12.9 0.0 copy-done.1
  12.9 1.9 %adjoint32.1 = (f32[224,128]{1,0:T(8,128)S(1)}, f32[512,256]{1,0:T(8,128)S(1)}) custom-call(f32[1,4]{1,0:T(1,128)S(1)} %bitcast.15, f32[64,432]{1,0:T(8,128)S(1)} %copy-done, bf16[2048,256]{1,0:T(8,128)(2,1)S(1)} %copy-done.3, bf16[2048,256]{1,0:T(8,128)(2,1)S(1)} %copy-done.2), custom_call_target="tpu_custom_call" | custom-call | flops 2000000000 | bytes 2000000 | tf_op jit(solution)/shard_map/adjoint32/pallas_call | solution.py:558
  14.8 6.2 %all-to-all-done = f32[16,2,8,128]{3,2,1,0:T(8,128)S(1)} async-done(((f32[16,2,8,128]{3,2,1,0:T(8,128)}), f32[16,2,8,128]{3,2,1,0:T(8,128)S(1)}, u32[]{:S(2)}, u32[]{:S(2)}) %all-to-all-start) | async-done | bytes 131104 | tf_op jit(solution)/shard_map/all_to_all | solution.py:583
  21.0 0.7 %forward1.1 = f32[448,128]{1,0:T(8,128)S(1)} custom-call(f32[256,128]{1,0:T(8,128)S(1)} %bitcast.13, bf16[2048,256]{1,0:T(8,128)(2,1)S(1)} %copy-done.3, bf16[2048,256]{1,0:T(8,128)(2,1)S(1)} %copy-done.2, f32[224,128]{1,0:T(8,128)S(1)} %get-tuple-element.6.other_ref, f32[512,256]{1,0:T(8,128)S(1)} %get-tuple-element.7.turn_ref), custom_call_target="tpu_custom_call" | custom-call | flops 1000000000 | bytes 2000000 | tf_op jit(solution)/shard_map/forward1/pallas_call | solution.py:558
  21.7 24.8 %all_to_all.15 = f32[32,7,2,128]{3,2,1,0:T(2,128)S(1)} all-to-all(f32[32,7,2,128]{3,2,1,0:T(2,128)S(1)} %bitcast.11), channel_id=1, replica_groups=mesh['sx'=16,'sy'=32] {'sy'}, dimensions={0} | all-to-all | bytes 458752 | tf_op jit(solution)/shard_map/all_to_all | solution.py:583
  46.4 1.5 %adjoint1.1 = f32[256,128]{1,0:T(8,128)} custom-call(f32[448,128]{1,0:T(8,128)S(1)} %bitcast.9, bf16[2048,256]{1,0:T(8,128)(2,1)S(1)} %copy-done.3, bf16[2048,256]{1,0:T(8,128)(2,1)S(1)} %copy-done.2, f32[512,256]{1,0:T(8,128)S(1)} %get-tuple-element.7.turn_ref), custom_call_target="tpu_custom_call" | custom-call | flops 1000000000 | bytes 2000000 | tf_op jit(solution)/shard_map/adjoint1/pallas_call | solution.py:558
  47.9 4.0 %all-to-all-start.2 = ((f32[16,2,8,128]{3,2,1,0:T(8,128)}), f32[16,2,8,128]{3,2,1,0:T(8,128)S(1)}, u32[]{:S(2)}, u32[]{:S(2)}) async-start(f32[16,2,8,128]{3,2,1,0:T(8,128)} %bitcast.6), calls=%async_computation.2 | async-start | bytes 262144 | tf_op jit(solution)/shard_map/all_to_all | solution.py:583
  51.9 2.7 %forward23.1 = (f32[64,432]{1,0:T(8,128)}, f32[192,256]{1,0:T(8,128)S(1)}) custom-call(f32[1,4]{1,0:T(1,128)S(1)} %bitcast.16, f32[448,128]{1,0:T(8,128)S(1)} %bitcast.10, bf16[2048,256]{1,0:T(8,128)(2,1)S(1)} %copy-done.3, bf16[2048,256]{1,0:T(8,128)(2,1)S(1)} %copy-done.2), custom_call_target="tpu_custom_call" | custom-call | flops 2000000000 | bytes 2000000 | tf_op jit(solution)/shard_map/forward23/pallas_call | solution.py:558
  54.6 5.9 %all-to-all-done.2 = f32[16,2,8,128]{3,2,1,0:T(8,128)S(1)} async-done(((f32[16,2,8,128]{3,2,1,0:T(8,128)}), f32[16,2,8,128]{3,2,1,0:T(8,128)S(1)}, u32[]{:S(2)}, u32[]{:S(2)}) %all-to-all-start.2) | async-done | bytes 131104 | tf_op jit(solution)/shard_map/all_to_all | solution.py:583
  60.5 1.6 %adjoint0.1 = f32[64,432]{1,0:T(8,128)} custom-call(f32[256,128]{1,0:T(8,128)S(1)} %bitcast.12, bf16[2048,256]{1,0:T(8,128)(2,1)S(1)} %copy-done.3, bf16[2048,256]{1,0:T(8,128)(2,1)S(1)} %copy-done.2, f32[192,256]{1,0:T(8,128)S(1)} %get-tuple-element.9.turn_ref), custom_call_target="tpu_custom_call" | custom-call | flops 1000000000 | bytes 2000000 | tf_op jit(solution)/shard_map/adjoint0/pallas_call | solution.py:558
Async XLA Ops:
  0.6 12.3 %copy-start.2 = (bf16[2048,256]{1,0:T(8,128)(2,1)S(1)}, bf16[2048,256]{1,0:T(8,128)(2,1)}, u32[]{:S(2)}) copy-start(bf16[2048,256]{1,0:T(8,128)(2,1)} %constant.5.clone.wl_ref) | copy-start | bytes 3145732
  0.6 12.3 %copy-start.3 = (bf16[2048,256]{1,0:T(8,128)(2,1)S(1)}, bf16[2048,256]{1,0:T(8,128)(2,1)}, u32[]{:S(2)}) copy-start(bf16[2048,256]{1,0:T(8,128)(2,1)} %constant.4.clone.wh_ref) | copy-start | bytes 3145732
  3.4 9.6 %copy-start = (f32[64,432]{1,0:T(8,128)S(1)}, f32[64,432]{1,0:T(8,128)}, u32[]{:S(2)}) copy-start(f32[64,432]{1,0:T(8,128)} %x_ref.1) | copy-start | bytes 331780
  3.4 9.6 %copy-start.1 = (f32[4]{0:T(128)S(1)}, f32[4]{0:T(128)}, u32[]{:S(2)}) copy-start(f32[4]{0:T(128)} %param.7) | copy-start | bytes 52
  3.4 17.6 %all-to-all-start = ((f32[16,2,8,128]{3,2,1,0:T(8,128)}), f32[16,2,8,128]{3,2,1,0:T(8,128)S(1)}, u32[]{:S(2)}, u32[]{:S(2)}) async-start(f32[16,2,8,128]{3,2,1,0:T(8,128)} %bitcast.17), calls=%async_computation | async-start | bytes 262144 | tf_op jit(solution)/shard_map/all_to_all | solution.py:583
  47.9 12.6 %all-to-all-start.2 = ((f32[16,2,8,128]{3,2,1,0:T(8,128)}), f32[16,2,8,128]{3,2,1,0:T(8,128)S(1)}, u32[]{:S(2)}, u32[]{:S(2)}) async-start(f32[16,2,8,128]{3,2,1,0:T(8,128)} %bitcast.6), calls=%async_computation.2 | async-start | bytes 262144 | tf_op jit(solution)/shard_map/all_to_all | solution.py:583
